TPU v7x, 512 devices: a whole 4x4x16 slice. The times are simulated.
512 devices in a mesh: ctx: 32 (over z, core), tp: 16 (over x, y).
Axes of the slice: x: 4, y: 4, z: 16, core: 2. Of those that a mesh axis runs over, the one named last changes fastest.
Arguments:
- teacher_span: bfloat16 [512, 8192], P('ctx', 'tp'), may hold values from -20 to 20
- teacher_context: bfloat16 [16384, 8192], P(('ctx', 'tp')), may hold values from -16 to 16
- student_span: bfloat16 [512, 2560], P('ctx', 'tp'), may hold values from -28 to 28
- student_context: bfloat16 [16384, 2560], P(('ctx', 'tp')), may hold values from -20 to 20
- query_weights: float32 [512], replicated, may hold values from 0.25 to 4
Outputs:
- grad_span: float32 [512, 2560], P('ctx', 'tp')
- grad_context: float32 [16384, 2560], P(('ctx', 'tp'))
All inputs are finite; a program needn't handle non-finite values.
Results may differ from a plain program's by a relative error of at most 0.0022.
Values may be sent and summed in bfloat16 or wider, within the bound.
No kernel may reach another device: no remote copies, remote signals or barrier semaphores. Data moves between devices by JAX's collectives and lax.ppermute only.
A program may use at most 64 MiB of HBM per device.

v0:
```python
import math

import jax
import jax.numpy as jnp
from jax import lax
from jax.sharding import PartitionSpec as P

TH = 128
SH = 40


def on_device(teacher_span, teacher_context, student_span, student_context, query_weights):
    teach_rows, stud_rows = (
        lax.all_gather(teacher_span, "ctx", axis=0, tiled=True),
        lax.all_gather(student_span, "ctx", axis=0, tiled=True),
    )
    teach_keys, stud_keys = (
        lax.all_to_all(teacher_context, "tp", split_axis=1, concat_axis=0, tiled=True),
        lax.all_to_all(student_context, "tp", split_axis=1, concat_axis=0, tiled=True),
    )
    local_heads = teach_rows.shape[1] // TH
    keys_total = teach_keys.shape[0] * lax.axis_size("ctx")
    row_coef = (math.sqrt(keys_total) * query_weights)[:, None]

    def head_scores(head_num):
        teach_score = jnp.einsum(
            "qd,kd->qk",
            teach_rows[:, head_num * TH : (head_num + 1) * TH],
            teach_keys[:, head_num * TH : (head_num + 1) * TH],
            preferred_element_type=jnp.float32,
        ) / math.sqrt(TH)
        stud_score = jnp.einsum(
            "qd,kd->qk",
            stud_rows[:, head_num * SH : (head_num + 1) * SH],
            stud_keys[:, head_num * SH : (head_num + 1) * SH],
            preferred_element_type=jnp.float32,
        ) / math.sqrt(SH)
        return (teach_score, stud_score)

    teach_maxes, teach_sums, stud_maxes, stud_sums = ([], [], [], [])
    for head_num in range(local_heads):
        teach_score, stud_score = head_scores(head_num)
        teach_top = jnp.max(teach_score, axis=1)
        stud_top = jnp.max(stud_score, axis=1)
        teach_maxes.append(teach_top)
        stud_maxes.append(stud_top)
        teach_sums.append(jnp.sum(jnp.exp(teach_score - teach_top[:, None]), axis=1))
        stud_sums.append(jnp.sum(jnp.exp(stud_score - stud_top[:, None]), axis=1))
    teach_max = jnp.stack(teach_maxes)
    teach_sum = jnp.stack(teach_sums)
    stud_max = jnp.stack(stud_maxes)
    stud_sum = jnp.stack(stud_sums)
    global_teach, global_stud = lax.pmax((teach_max, stud_max), "ctx")
    teach_sum, stud_sum = lax.psum(
        (teach_sum * jnp.exp(teach_max - global_teach), stud_sum * jnp.exp(stud_max - global_stud)),
        "ctx",
    )
    teach_max, stud_max = (global_teach, global_stud)
    grad_list, key_parts, query_parts = ([], [], [])
    for head_num in range(local_heads):
        teach_score, stud_score = head_scores(head_num)
        teach_prob = (
            jnp.exp(teach_score - teach_max[head_num][:, None]) / teach_sum[head_num][:, None]
        )
        stud_prob = jnp.exp(stud_score - stud_max[head_num][:, None]) / stud_sum[head_num][:, None]
        grad_score = (row_coef * (stud_prob - teach_prob)).astype(jnp.bfloat16)
        stud_query = stud_rows[:, head_num * SH : (head_num + 1) * SH]
        key_parts.append(
            jnp.einsum("qk,qd->kd", grad_score, stud_query, preferred_element_type=jnp.float32)
            / math.sqrt(SH)
        )
        query_parts.append(
            jnp.dot(
                grad_score,
                stud_keys[:, head_num * SH : (head_num + 1) * SH],
                preferred_element_type=jnp.float32,
            )
            / math.sqrt(SH)
        )
    key_part = jnp.concatenate(key_parts, axis=1)
    grad_context = lax.all_to_all(key_part, "tp", split_axis=0, concat_axis=1, tiled=True)
    grad_span = lax.psum_scatter(
        jnp.concatenate(query_parts, axis=1), "ctx", scatter_dimension=0, tiled=True
    )
    return (grad_span, grad_context)


def solution(mesh):
    placed = (P("ctx", "tp"), P(("ctx", "tp"), None), P("ctx", "tp"), P(("ctx", "tp"), None), P())
    return jax.shard_map(
        on_device,
        mesh=mesh,
        in_specs=placed,
        out_specs=(P("ctx", "tp"), P(("ctx", "tp"), None)),
        check_vma=False,
    )
```

profile of v0, /device:TPU:1, one launch (start us, length us, event | category | flops | bytes accessed | tf_op | source)
XLA Modules:
  0.0 404.6 jit_solution(11303405608241154407)
XLA Ops:
  7.2 1.2 all_to_all.42
  8.4 0.8 copy.17
  9.2 7.6 %all-to-all-start = ((bf16[32,16,160]{2,0,1:T(8,128)(2,1)}), bf16[32,16,160]{2,0,1:T(8,128)(2,1)S(1)}, u32[]{:S(2)}, u32[]{:S(2)}) async-start(bf16[32,16,160]{2,0,1:T(8,128)(2,1)} %copy.17), calls=%async_computation | async-start | bytes 524288 | tf_op jit(solution)/shard_map/all_to_all | solution.py:19
  16.8 0.9 copy.26
  17.7 41.2 %all_gather.7 = bf16[512,512]{1,0:T(8,128)(2,1)} all-gather(bf16[16,512]{1,0:T(8,128)(2,1)S(1)} %copy-done.14), channel_id=1, replica_groups=mesh['ctx'=32,'tp'=16] {'ctx'}, dimensions={0}, use_global_device_ids=true | all-gather | bytes 540672 | tf_op jit(solution)/shard_map/all_gather | solution.py:14
  58.9 27.9 %all_gather.6 = bf16[512,160]{1,0:T(8,128)(2,1)S(1)} all-gather(bf16[16,160]{1,0:T(8,128)(2,1)S(1)} %copy-done.15), channel_id=1, replica_groups=mesh['ctx'=32,'tp'=16] {'ctx'}, dimensions={0}, use_global_device_ids=true | all-gather | bytes 168960 | tf_op jit(solution)/shard_map/all_gather | solution.py:15
  86.9 7.0 %all-to-all-start.1 = ((bf16[32,16,512]{2,0,1:T(8,128)(2,1)}), bf16[32,16,512]{2,0,1:T(8,128)(2,1)}, u32[]{:S(2)}, u32[]{:S(2)}) async-start(bf16[32,16,512]{2,0,1:T(8,128)(2,1)} %bitcast.52), calls=%async_computation.1 | async-start | bytes 1048576 | tf_op jit(solution)/shard_map/all_to_all | solution.py:18
  93.9 0.4 fusion.32
  94.3 0.4 fusion.33
  94.7 0.4 fusion.34
  95.1 1.2 fusion.35
  97.1 7.0 %all-to-all-done.1 = bf16[32,16,512]{2,0,1:T(8,128)(2,1)} async-done(((bf16[32,16,512]{2,0,1:T(8,128)(2,1)}), bf16[32,16,512]{2,0,1:T(8,128)(2,1)}, u32[]{:S(2)}, u32[]{:S(2)}) %all-to-all-start.1) | async-done | bytes 524320 | tf_op jit(solution)/shard_map/all_to_all | solution.py:18
  104.1 1.3 fusion.28
  105.5 1.4 fusion.29
  106.8 1.4 fusion.30
  108.2 1.4 fusion.31
  110.2 0.4 copy-done.5
  110.8 88.8 %all-reduce.1 = (f32[4,512]{1,0:T(4,128)S(1)}, f32[4,512]{1,0:T(4,128)S(1)}) all-reduce(f32[4,512]{1,0:T(4,128)S(1)} %pad_maximum_fusion.3, f32[4,512]{1,0:T(4,128)S(1)} %pad_maximum_fusion.2), channel_id=1, replica_groups=mesh['ctx'=32,'tp'=16] {'ctx'}, use_global_device_ids=true, to_apply=%region_14.0 | all-reduce | flops 4096 | bytes 32768 | tf_op jit(solution)/shard_map/pmax | solution.py:53
  199.6 90.0 %all-reduce = (f32[4,512]{1,0:T(4,128)S(1)}, f32[4,512]{1,0:T(4,128)S(1)}) all-reduce(f32[4,512]{1,0:T(4,128)S(1)} %get-tuple-element.50, f32[4,512]{1,0:T(4,128)S(1)} %get-tuple-element.49), channel_id=1, replica_groups=mesh['ctx'=32,'tp'=16] {'ctx'}, use_global_device_ids=true, to_apply=%region_19.0 | all-reduce | flops 4096 | bytes 32768 | tf_op jit(solution)/shard_map/psum | solution.py:54
  289.7 2.1 multiply_convert_fusion
  291.8 0.3 convolution_multiply_fusion.12
  292.1 0.3 convolution_multiply_fusion.8
  292.5 0.6 copy-done.2
  293.0 1.1 multiply_convert_fusion.3
  294.2 0.3 convolution_multiply_fusion.13
  294.5 0.3 convolution_multiply_fusion.9
  295.1 0.3 convolution_multiply_fusion.10
  295.8 1.0 copy.22
  297.3 12.4 %all_to_all.57 = f32[16,32,160]{2,1,0:T(8,128)S(1)} all-to-all(f32[16,32,160]{2,1,0:T(8,128)S(1)} %bitcast.61), channel_id=1, replica_groups=mesh['ctx'=32,'tp'=16] {'tp'}, dimensions={0} | all-to-all | bytes 655360 | tf_op jit(solution)/shard_map/all_to_all | solution.py:81
  309.7 0.3 copy.20
  310.0 1.0 all_to_all.53
  311.0 86.7 %reduce-scatter.4.cloned.1.call-done = f32[16,160]{1,0:T(8,128)} async-done(((f32[512,160]{1,0:T(8,128)}), f32[16,160]{1,0:T(8,128)}) %reduce-scatter.4.cloned.1.call-update) | async-done | bytes 10256
  (56 shorter events, 2.9 us)
Async XLA Ops:
  8.4 8.4 %copy-start.13 = (bf16[32,8192]{1,0:T(8,128)(2,1)S(1)}, bf16[32,8192]{1,0:T(8,128)(2,1)}, u32[]{:S(2)}) copy-start(bf16[32,8192]{1,0:T(8,128)(2,1)} %param.6) | copy-start | bytes 1572868
  9.2 77.6 %all-to-all-start = ((bf16[32,16,160]{2,0,1:T(8,128)(2,1)}), bf16[32,16,160]{2,0,1:T(8,128)(2,1)S(1)}, u32[]{:S(2)}, u32[]{:S(2)}) async-start(bf16[32,16,160]{2,0,1:T(8,128)(2,1)} %copy.17), calls=%async_computation | async-start | bytes 524288 | tf_op jit(solution)/shard_map/all_to_all | solution.py:19
  16.8 0.9 copy-start.14
  17.7 41.2 %copy-start.15 = (bf16[16,160]{1,0:T(8,128)(2,1)S(1)}, bf16[16,160]{1,0:T(8,128)(2,1)}, u32[]{:S(2)}) copy-start(bf16[16,160]{1,0:T(8,128)(2,1)} %param.7) | copy-start | bytes 15364
  58.9 27.9 %copy-start.16 = (f32[512]{0:T(512)S(1)}, f32[512]{0:T(512)}, u32[]{:S(2)}) copy-start(f32[512]{0:T(512)} %param.9) | copy-start | bytes 6148
  86.8 7.9 %copy-start.8 = (bf16[32,16,160]{2,0,1:T(8,128)(2,1)}, bf16[32,16,160]{2,0,1:T(8,128)(2,1)S(1)}, u32[]{:S(2)}) copy-start(bf16[32,16,160]{2,0,1:T(8,128)(2,1)S(1)} %all-to-all-done) | copy-start | bytes 491524
  86.9 17.2 %all-to-all-start.1 = ((bf16[32,16,512]{2,0,1:T(8,128)(2,1)}), bf16[32,16,512]{2,0,1:T(8,128)(2,1)}, u32[]{:S(2)}, u32[]{:S(2)}) async-start(bf16[32,16,512]{2,0,1:T(8,128)(2,1)} %bitcast.52), calls=%async_computation.1 | async-start | bytes 1048576 | tf_op jit(solution)/shard_map/all_to_all | solution.py:18
  93.9 303.9 %reduce-scatter.4.cloned.1.call-start = ((), (), s32[]{:S(2)}) async-start(), calls=%async_computation.4 | async-start | bytes 540672
  94.3 2.0 copy-start
  104.1 1.3 copy-start.12
  105.4 4.2 %copy-start.7 = (f32[512,512]{0,1:T(8,128)}, f32[512,512]{0,1:T(8,128)S(1)}, u32[]{:S(2)}) copy-start(f32[512,512]{0,1:T(8,128)S(1)} %get-tuple-element.34) | copy-start | bytes 3145732
  106.8 3.0 copy-start.1
  108.2 1.8 copy-start.3
  109.6 1.0 copy-start.5
  289.7 2.1 copy-start.9
  289.7 2.8 copy-start.4
  289.7 2.8 copy-start.6
  291.8 1.3 copy-start.2
  294.2 1.3 copy-start.10
  295.8 1.0 copy-start.11
Sparse Core Ops, SparseCore 0:
  296.9 100.7 reduce-scatter.3
where the time goes:
time: 407 us; the launch traced here: 405 us
  blocking collectives  260 us (64%)
  waiting for transfers between devices  93.7 us (23%)
  starting transfers between devices  14.6 us (4%)
  between operations  14.4 us (4%)
  matrix products  10.2 us (3%)
  local copies, waits for them, and re-layouts  6.42 us (2%)
  other arithmetic  4.89 us (1%)
    psum x1, blocking collectives, on_device(): lax.psum((teach_sum * jnp.exp(teach_max - global_teach), stud_sum * jnp.e...  90 us
    pmax x1, blocking collectives, on_device(): global_teach, global_stud = lax.pmax((teach_max, stud_max), 'ctx')  88.8 us
    unnamed x2, waiting for transfers between devices  86.7 us
    all_gather x1, blocking collectives, on_device(): lax.all_gather(teacher_span, 'ctx', axis=0, tiled=True)  41.2 us
    all_gather x1, blocking collectives, on_device(): lax.all_gather(student_span, 'ctx', axis=0, tiled=True)  27.9 us
    all_to_all x1, blocking collectives, on_device(): lax.all_to_all(key_part, 'tp', split_axis=0, concat_axis=1, tiled=True)  12.4 us
  transfers between devices with their start and end apart: 3, of which 2 were waited for; matrix products, arithmetic and copies ran while one was open for 1% of the time, Pallas kernels for 0%

commit v1 on v0

v1 whole, which is shorter than its diff:
```python
import functools
import math

import jax
import jax.numpy as jnp
from jax import lax
from jax.experimental import pallas as pl
from jax.experimental.pallas import tpu as pltpu
from jax.sharding import Mesh, PartitionSpec as P

TH = 128
SH = 40
CORES = 2
NEAR = 2
LANES = 128
HALF = LANES // 2
LOG2E = math.log2(math.e)
F32 = jnp.float32
BF16 = jnp.bfloat16


def side_by_side(low, high):
    gap = jnp.zeros((low.shape[0], HALF - SH), low.dtype)
    return jnp.concatenate([low, gap, high, gap], axis=1)


def pack(side_ref, tq_hbm, tk_hbm, sq_hbm, sk_hbm, keys_hbm, kept_ref, given_ref,
         tq_ref, tk_ref, sq_ref, sk_ref, keys_ref, sems):
    heads, tokens, half = keys_hbm.shape[0], tk_hbm.shape[0], tk_hbm.shape[0] // 2
    fetches = [
        pltpu.make_async_copy(source, target, sems.at[number])
        for number, (source, target) in enumerate(
            [(tq_hbm, tq_ref), (sq_hbm, sq_ref), (sk_hbm, sk_ref), (tk_hbm, tk_ref)]
        )
    ]
    for copy in fetches:
        copy.start()
    rows = tq_ref.shape[0]

    def fill(out_ref, second):
        teach = [tq_ref[:, head * TH : (head + 1) * TH] for head in range(NEAR * CORES)]
        out_ref[:rows, :] = jnp.where(second, teach[1], teach[0])
        out_ref[rows : 2 * rows, :] = jnp.where(second, teach[2], teach[3])
        stud = [sq_ref[:, head * SH : (head + 1) * SH] for head in range(NEAR * CORES)]
        out_ref[2 * rows :, :] = jnp.where(
            second, side_by_side(stud[1], stud[2]), side_by_side(stud[0], stud[3])
        )

    fetches[0].wait()
    fetches[1].wait()
    second = side_ref[0] == 1
    fill(kept_ref, second)
    fill(given_ref, jnp.logical_not(second))
    fetches[2].wait()
    for head in range(heads):
        part = sk_ref[:, head * SH : (head + 1) * SH]
        keys_ref[head, tokens:, :] = side_by_side(part[:half], part[half:])
    fetches[3].wait()
    group = heads // 4
    sends = []
    for start in range(0, heads, group):
        for head in range(start, start + group):
            keys_ref[head, :tokens, :] = tk_ref[:, head * TH : (head + 1) * TH]
        here = pl.ds(start, group)
        sends.append(
            pltpu.make_async_copy(keys_ref.at[here], keys_hbm.at[here], sems.at[4 + start // group])
        )
        sends[-1].start()
    for copy in sends:
        copy.wait()


def queries_of(near_ref, rows_ref):
    count, deep, lanes = rows_ref.shape
    own = deep // (NEAR + 1)
    near = near_ref[0]
    start = pl.multiple_of(near * own, own)
    teach = rows_ref[:, pl.ds(start, own), :].reshape(count * own, lanes)
    stud = rows_ref[:, NEAR * own :, :].reshape(count * own, lanes).astype(F32)
    turned = jnp.concatenate([stud[:, HALF:], stud[:, :HALF]], axis=1)
    low = lax.broadcasted_iota(jnp.int32, (1, lanes), 1) < HALF
    first = near == 0
    left = jnp.where(low, jnp.where(first, stud, turned), 0.0)
    right = jnp.where(low, 0.0, jnp.where(first, turned, stud))
    return teach, left.astype(BF16), right.astype(BF16)


def key_chunk(keys_ref, start, size):
    part = keys_ref[pl.ds(start, size)]
    own = part.shape[1] // 3
    flat = lambda block: block.reshape(size * own, LANES)
    return flat(part[:, :own]), flat(part[:, own : 2 * own]), flat(part[:, 2 * own :])


def scores_of(span, key):
    return lax.dot_general(key, span, (((1,), (1,)), ((), ())), preferred_element_type=F32)


def turn(array):
    return jnp.concatenate([array[..., HALF:], array[..., :HALF]], axis=-1)


def low_lanes(rank):
    shape = (1,) * (rank - 1) + (LANES,)
    return lax.broadcasted_iota(jnp.int32, shape, rank - 1) < HALF


def totals_kernel(chunk, near_ref, keys_ref, rows_ref, out_ref, span_ref, score_ref):
    teach_q, left_q, right_q = queries_of(near_ref, rows_ref)
    span_ref[0], span_ref[1], span_ref[2] = teach_q, left_q, right_q
    queries = teach_q.shape[0]
    steps = keys_ref.shape[0] // chunk
    scales = (LOG2E / math.sqrt(TH), LOG2E / math.sqrt(SH))

    def measure(index, tops):
        first, second, pack = key_chunk(keys_ref, index * chunk, chunk)
        here = pl.ds(index * first.shape[0], first.shape[0])
        found = []
        for kind, span, key in ((0, 0, first), (0, 0, second), (1, 1, pack), (1, 2, pack)):
            score = scores_of(span_ref[span], key)
            score_ref[len(found), here] = score
            found.append(jnp.max(score.reshape(-1, 8, queries), axis=0))
        return jnp.maximum(tops[0], jnp.maximum(found[0], found[1])), jnp.maximum(
            tops[1], jnp.maximum(found[2], found[3])
        )

    start = jnp.full((8, queries), -1e30, F32)
    tops = lax.fori_loop(0, steps, measure, (start, start), unroll=True)
    tops = [jnp.max(top, axis=0, keepdims=True) * scale for top, scale in zip(tops, scales)]

    def gather(index, state):
        sums, means = list(state[:2]), state[2]
        _, _, pack = key_chunk(keys_ref, index * chunk, chunk)
        here = pl.ds(index * pack.shape[0], pack.shape[0])
        low = low_lanes(2)
        none = jnp.zeros_like(pack)
        turned = turn(pack.astype(F32)).astype(BF16)
        keys = (
            jnp.where(low, pack, none),
            jnp.where(low, turned, none),
            jnp.where(low, none, turned),
            jnp.where(low, none, pack),
        )
        left, right = [], []
        for number in range(4):
            kind = number // 2
            prob = jnp.exp2(score_ref[number, here] * scales[kind] - tops[kind])
            sums[kind] = sums[kind] + jnp.sum(prob.reshape(-1, 8, queries), axis=0)
            high = prob.astype(BF16)
            left += [keys[number], keys[number]]
            right += [high, (prob - high.astype(F32)).astype(BF16)]
        means = means + lax.dot_general(
            jnp.concatenate(left, axis=0),
            jnp.concatenate(right, axis=0),
            (((0,), (0,)), ((), ())),
            preferred_element_type=F32,
        )
        return sums[0], sums[1], means

    none = jnp.zeros((8, queries), F32)
    state = lax.fori_loop(
        0, steps, gather, (none, none, jnp.zeros((LANES, queries), F32)), unroll=True
    )
    lines, columns = [], []
    for kind in range(2):
        total = jnp.sum(state[kind], axis=0, keepdims=True)
        log = tops[kind] + jnp.log2(total)
        lines += [log[:, k : k + LANES] for k in range(0, queries, LANES)]
        mean = state[2][kind * HALF : kind * HALF + SH] * (1.0 / total)
        columns += [mean, jnp.broadcast_to(log, (HALF - SH, queries))]
    groups, own = out_ref.shape[0], out_ref.shape[1] - 8
    out_ref[:, :own, :] = jnp.concatenate(columns, axis=0).T.reshape(groups, own, LANES)
    out_ref[:, own:, :] = jnp.broadcast_to(
        jnp.concatenate(lines, axis=0)[None], (groups, 8, LANES)
    )


def grads_kernel(
    chunk, near_ref, logs_ref, weights_ref, own_ref, keys_ref, rows_ref, key_ref, span_ref
):
    deep = logs_ref.shape[1] - 8
    logs = logs_ref[:, deep:, :]
    high = jnp.max(logs, axis=0)
    logs = high + jnp.log2(jnp.sum(jnp.exp2(logs - high[None]), axis=0))
    lines = logs.shape[0] // 2
    flat = lambda rows: jnp.concatenate([rows[k : k + 1] for k in range(lines)], axis=1)
    teach_log, stud_log = flat(logs[:lines]), flat(logs[lines:])
    weights = weights_ref[...]
    teach_q, left_q, right_q = queries_of(near_ref, rows_ref)
    span_ref[0], span_ref[1], span_ref[2] = teach_q, left_q, right_q
    own = key_ref.shape[1] // 2

    means = logs_ref[:, :deep, :]
    each = jnp.where(low_lanes(3), means[:, :, SH : SH + 1], means[:, :, HALF + SH : HALF + SH + 1])
    share = jnp.exp2(each - jnp.max(each, axis=0, keepdims=True))
    mean = jnp.sum(share * means, axis=0) / jnp.sum(share, axis=0)
    mean = (turn(mean) - mean) * own_ref[...] * (1.0 / math.sqrt(SH))
    rough = mean.astype(BF16).astype(F32)
    mean = jnp.where(low_lanes(2), rough, turn(mean - rough)).astype(BF16)
    for head in range(key_ref.shape[0]):
        start = head % (deep // own) * own
        key_ref[head, own:, :] = mean[start : start + own]

    def grad(teach_score, stud_score):
        teach = jnp.exp2(teach_score * (LOG2E / math.sqrt(TH)) - teach_log)
        stud = jnp.exp2(stud_score * (LOG2E / math.sqrt(SH)) - stud_log)
        return (weights * (stud - teach)).astype(BF16)

    def step(index, _):
        first, second, pack = key_chunk(keys_ref, index * chunk, chunk)
        left = grad(scores_of(span_ref[0], first), scores_of(span_ref[1], pack))
        right = grad(scores_of(span_ref[0], second), scores_of(span_ref[2], pack))
        mix = jnp.dot(left, span_ref[1], preferred_element_type=F32)
        mix = mix + jnp.dot(right, span_ref[2], preferred_element_type=F32)
        mix = (mix * (1.0 / math.sqrt(SH))).astype(key_ref.dtype)
        key_ref[pl.ds(index * chunk, chunk), :own, :] = mix.reshape(chunk, own, LANES)
        return 0

    lax.fori_loop(0, keys_ref.shape[0] // chunk, step, 0, unroll=True)


def unpack(tp_ref, in_ref, context_ref, span_ref):
    half = in_ref.shape[1] // 2
    group = 16
    for start in range(0, in_ref.shape[0], group):
        for side in range(2):
            parts = [
                in_ref[head, :half, side * HALF : side * HALF + SH].astype(F32)
                for head in range(start, start + group)
            ]
            context_ref[side * half : (side + 1) * half, start * SH : (start + group) * SH] = (
                jnp.concatenate(parts, axis=1)
            )
    near = NEAR * CORES
    rows = in_ref[pl.ds(tp_ref[0] * near, near), half:, :].astype(F32)
    rows = rows + turn(rows)
    span_ref[...] = jnp.concatenate([rows[head, :, :SH] for head in range(near)], axis=1)


def call(body, shapes, scratch=(), smem=0, raw=0, raw_out=0, flops=0, room=48):
    kinds = [pltpu.SMEM, pltpu.HBM, pltpu.VMEM]
    specs = lambda counts: [
        pl.BlockSpec(memory_space=kind) for kind, count in zip(kinds, counts) for _ in range(count)
    ]

    def run(*args):
        many = isinstance(shapes, (list, tuple))
        outs = specs((0, raw_out, (len(shapes) if many else 1) - raw_out))
        moved = sum(arg.size * arg.dtype.itemsize for arg in args)
        return pl.pallas_call(
            body,
            out_shape=shapes,
            in_specs=specs((smem, raw, len(args) - smem - raw)),
            out_specs=outs if many else outs[0],
            scratch_shapes=list(scratch),
            cost_estimate=pl.CostEstimate(flops=flops, bytes_accessed=moved, transcendentals=0),
            compiler_params=pltpu.CompilerParams(vmem_limit_bytes=room * 2**20),
        )(*args)

    return run


def on_device(teacher_span, teacher_context, student_span, student_context, query_weights):
    groups, tps = lax.axis_size("group"), lax.axis_size("tp")
    heads = tps * NEAR * CORES
    near = NEAR * CORES
    rows_own, tokens_own = teacher_span.shape[0], teacher_context.shape[0]
    half = tokens_own // 2
    queries = query_weights.shape[0]
    shape = jax.ShapeDtypeStruct

    def trade(array, axes):
        return lax.all_to_all(array, axes, split_axis=0, concat_axis=0, tiled=True)

    core, spot = lax.axis_index("core"), lax.axis_index("near").astype(jnp.int32).reshape(1)
    piece = shape(((NEAR + 1) * rows_own, LANES), BF16)
    keys, kept, given = call(
        pack,
        (shape((heads, 3 * half, LANES), BF16), piece, piece),
        scratch=[
            pltpu.VMEM(teacher_span.shape, BF16),
            pltpu.VMEM(teacher_context.shape, BF16),
            pltpu.VMEM(student_span.shape, BF16),
            pltpu.VMEM(student_context.shape, BF16),
            pltpu.VMEM((heads, 3 * half, LANES), BF16),
            pltpu.SemaphoreType.DMA((8,)),
        ],
        smem=1,
        raw=4,
        raw_out=1,
        room=62,
    )(
        (spot[0] ^ core).astype(jnp.int32).reshape(1),
        teacher_span,
        teacher_context,
        student_span,
        student_context,
    )
    other = lax.ppermute(given, "core", [(0, 1), (1, 0)])
    order = lambda first, second: jnp.stack(
        [part.reshape(NEAR + 1, rows_own, LANES) for part in (first, second)], axis=1
    )
    shard = jnp.where(core == 0, order(kept, other), order(other, kept))
    shard = shard.reshape(1, (NEAR + 1) * CORES * rows_own, LANES)
    keys = trade(keys, ("tp", "near", "core"))
    rows = lax.all_gather(
        shard,
        ("group", "near", "core"),
        axis=0,
        tiled=True,
        axis_index_groups=[
            [z * CORES + (z + side) % CORES for z in range(groups * NEAR)] for side in range(CORES)
        ],
    )

    spans = pltpu.VMEM((3, queries, LANES), BF16)
    deep = queries // groups
    logs = call(
        functools.partial(totals_kernel, 8),
        shape((groups, deep + 8, LANES), F32),
        scratch=[spans, pltpu.VMEM((4, heads * half, queries), F32)],
        smem=1,
        flops=2**31,
    )(spot, keys, rows)
    logs = trade(logs, "group")
    tokens_all = tokens_own * heads * groups
    weights = math.sqrt(tokens_all) * query_weights
    own = lax.dynamic_slice(weights, (lax.axis_index("group") * deep,), (deep,))
    own = jnp.broadcast_to(own[:, None], (deep, LANES))
    parts = call(
        functools.partial(grads_kernel, 8),
        shape((heads, 2 * half, LANES), BF16),
        scratch=[spans],
        smem=1,
        flops=2**30,
    )(spot, logs, weights.reshape(1, queries), own, keys, rows)
    parts = trade(parts, ("tp", "near", "core"))
    grad_context, grad_span = call(
        unpack, (shape((tokens_own, heads * SH), F32), shape((rows_own, near * SH), F32)), smem=1
    )(lax.axis_index("tp").astype(jnp.int32).reshape(1), parts)
    return (grad_span, grad_context)


def solution(mesh):
    ctx, tp = mesh.devices.shape
    split = Mesh(
        mesh.devices.reshape(ctx // (NEAR * CORES), NEAR, CORES, tp),
        ("group", "near", "core", "tp"),
    )
    rows = ("group", "near", "core")
    tokens = rows + ("tp",)
    placed = (P(rows, "tp"), P(tokens, None), P(rows, "tp"), P(tokens, None), P())
    return jax.shard_map(
        on_device,
        mesh=split,
        in_specs=placed,
        out_specs=(P(rows, "tp"), P(tokens, None)),
        check_vma=False,
    )
```

time: 407 us -> 113 us (0.28)
  blocking collectives: 260 us -> 34.7 us
  waiting for transfers between devices: 93.7 us -> 32 us
  starting transfers between devices: 14.6 us -> 31.7 us
  between operations: 14.4 us -> 0.72 us
  Pallas kernels: 0 us -> 12.8 us
  matrix products: 10.2 us -> 0 us
  local copies, waits for them, and re-layouts: 6.42 us -> 0.84 us
  other arithmetic: 4.89 us -> 0.01 us
    psum x1 -> x0, blocking collectives: 90 us -> none  [on_device(): lax.psum((teach_sum * jnp.exp(teach_max - global_teach), stud_sum * jnp.e...]
    pmax x1 -> x0, blocking collectives: 88.8 us -> none  [on_device(): global_teach, global_stud = lax.pmax((teach_max, stud_max), 'ctx')]
    unnamed x2 -> x0, waiting for transfers between devices: 86.7 us -> none
    all_gather x2 -> x1, blocking collectives: 69.1 us -> 34.7 us  [on_device(): lax.all_gather(shard, ('group', 'near', 'core'), axis=0, tiled=True, axis...]
    all_to_all x2 -> x3, waiting for transfers between devices: 6.96 us -> 31.2 us  [trade(): return lax.all_to_all(array, axes, split_axis=0, concat_axis=0, tiled=True)]
    all_to_all x2 -> x3, starting transfers between devices: 14.6 us -> 29.2 us  [trade(): return lax.all_to_all(array, axes, split_axis=0, concat_axis=0, tiled=True)]
    pallas_call x0 -> x4, Pallas kernels: none -> 12.8 us  [run(): pl.pallas_call(body, out_shape=shapes, in_specs=specs((smem, raw, len(arg...]
    all_to_all x1 -> x0, blocking collectives: 12.4 us -> none  [on_device(): lax.all_to_all(key_part, 'tp', split_axis=0, concat_axis=1, tiled=True)]
  transfers between devices with their start and end apart: 3 -> 4, of which waited for: 2 -> 3; matrix products, arithmetic and copies ran while one was open for 1% -> 0% of each run, Pallas kernels for 0% -> 0%
where the time goes in v1:
time: 113 us
  blocking collectives  34.7 us (31%)
  waiting for transfers between devices  32 us (28%)
  starting transfers between devices  31.7 us (28%)
  Pallas kernels  12.8 us (11%)
    all_gather x1, blocking collectives, on_device(): lax.all_gather(shard, ('group', 'near', 'core'), axis=0, tiled=True, axis...  34.7 us
    all_to_all x3, waiting for transfers between devices, trade(): return lax.all_to_all(array, axes, split_axis=0, concat_axis=0, tiled=True)  31.2 us
    all_to_all x3, starting transfers between devices, trade(): return lax.all_to_all(array, axes, split_axis=0, concat_axis=0, tiled=True)  29.2 us
    pallas_call x4, Pallas kernels, run(): pl.pallas_call(body, out_shape=shapes, in_specs=specs((smem, raw, len(arg...  12.8 us
    ppermute x1, starting transfers between devices, on_device(): other = lax.ppermute(given, 'core', [(0, 1), (1, 0)])  2.48 us
  transfers between devices with their start and end apart: 4, of which 3 were waited for; matrix products, arithmetic and copies ran while one was open for 0% of the time, Pallas kernels for 0%

profile of v1, /device:TPU:1, one launch (start us, length us, event | category | flops | bytes accessed | tf_op | source)
XLA Modules:
  0.0 112.8 jit_solution(3032319592051960256)
XLA Ops:
  0.6 2.8 %shard_map.68 = (bf16[64,48,128]{2,1,0:T(8,128)(2,1)}, bf16[48,128]{1,0:T(8,128)(2,1)}, bf16[48,128]{1,0:T(8,128)(2,1)}) custom-call(s32[1]{0:T(128)} %bitcast.2.side_ref, bf16[16,512]{1,0:T(8,128)(2,1)} %tq_hbm.1, bf16[32,8192]{1,0:T(8,128)(2,1)} %tk_hbm.1, bf16[16,160]{1,0:T(8,128)(2,1)} %sq_hbm.1, bf16[32,2560]{1,0:T(8,128)(2,1)} %sk_hbm.1), custom_call_target="tpu_custom_call" | custom-call | bytes 709636 | tf_op jit(solution)/shard_map/pallas_call | solution.py:250
  3.4 0.0 copy-start.2
  3.4 0.0 copy-start
  3.4 11.0 %all-to-all-start = ((bf16[64,48,128]{2,1,0:T(8,128)(2,1)}), bf16[64,48,128]{2,1,0:T(8,128)(2,1)S(1)}, u32[]{:S(2)}, u32[]{:S(2)}) async-start(bf16[64,48,128]{2,1,0:T(8,128)(2,1)} %get-tuple-element.7), calls=%async_computation | async-start | bytes 1572864 | tf_op jit(solution)/shard_map/all_to_all | solution.py:273
  14.4 0.0 copy-done.2
  14.4 2.5 %collective-permute-start = (bf16[48,128]{1,0:T(8,128)(2,1)S(1)}, bf16[48,128]{1,0:T(8,128)(2,1)S(1)}, u32[]{:S(2)}, u32[]{:S(2)}) collective-permute-start(bf16[48,128]{1,0:T(8,128)(2,1)S(1)} %copy-done.2), channel_id=1, source_target_pairs={{0,16},{16,0},{1,17},{17,1},{2,18},{18,2},{3,19},{19,3},{4,20},{20... | collective-permute-start | bytes 36872 | tf_op jit(solution)/shard_map/ppermute | solution.py:299
  16.9 0.8 collective-permute-done
  17.7 0.0 copy-done
  17.7 34.7 %all_gather.3.rows_ref = bf16[16,96,128]{2,1,0:T(8,128)(2,1)S(1)} all-gather(bf16[1,96,128]{2,1,0:T(8,128)(2,1)S(1)} %bitcast.8), channel_id=1, replica_groups={{0,48,64,112,128,176,192,240,256,304,320,368,384,432,448,496},{16,32,80..., dimensions={0}, use_global_device_ids=true | all-gather | bytes 417792 | tf_op jit(solution)/shard_map/all_gather | solution.py:306
  52.4 0.0 all-to-all-done.keys_ref
  52.4 5.3 %shard_map.69 = f32[8,72,128]{2,1,0:T(8,128)} custom-call(s32[1]{0:T(128)} %bitcast.1.near_ref, bf16[64,48,128]{2,1,0:T(8,128)(2,1)S(1)} %all-to-all-done.keys_ref, bf16[16,96,128]{2,1,0:T(8,128)(2,1)S(1)} %all_gather.3.rows_ref), custom_call_target="tpu_custom_call" | custom-call | flops 2147483648 | bytes 1179652 | tf_op jit(solution)/shard_map/pallas_call | solution.py:250
  57.7 6.5 %all-to-all-start.1 = ((f32[8,72,128]{2,1,0:T(8,128)}), f32[8,72,128]{2,1,0:T(8,128)S(1)}, u32[]{:S(2)}, u32[]{:S(2)}) async-start(f32[8,72,128]{2,1,0:T(8,128)} %shard_map.69), calls=%async_computation.1 | async-start | bytes 589824 | tf_op jit(solution)/shard_map/all_to_all | solution.py:273
  64.2 0.0 copy-start.1
  64.2 0.7 copy-done.1
  64.9 0.1 dynamic_slice.3
  65.0 18.4 %all-to-all-done.1.logs_ref = f32[8,72,128]{2,1,0:T(8,128)S(1)} async-done(((f32[8,72,128]{2,1,0:T(8,128)}), f32[8,72,128]{2,1,0:T(8,128)S(1)}, u32[]{:S(2)}, u32[]{:S(2)}) %all-to-all-start.1) | async-done | bytes 294944 | tf_op jit(solution)/shard_map/all_to_all | solution.py:273
  83.3 0.1 broadcast_in_dim.2.own_ref
  83.4 3.8 %shard_map.70 = bf16[64,32,128]{2,1,0:T(8,128)(2,1)} custom-call(s32[1]{0:T(128)} %bitcast.1.near_ref, f32[8,72,128]{2,1,0:T(8,128)S(1)} %all-to-all-done.1.logs_ref, f32[1,512]{1,0:T(1,128)S(1)} %bitcast.7, f32[64,128]{1,0:T(8,128)S(1)} %broadcast_in_dim.2.own_ref, bf16[64,48,128]{2,1,0:T(8,128)(2,1)S(1)} %all-to-all-done.keys_ref, ...), custom_call_target="tpu_custom_call" | custom-call | flops 1073741824 | bytes 1509380 | tf_op jit(solution)/shard_map/pallas_call | solution.py:250
  87.2 11.8 %all-to-all-start.2 = ((bf16[64,32,128]{2,1,0:T(8,128)(2,1)}), bf16[64,32,128]{2,1,0:T(8,128)(2,1)S(1)}, u32[]{:S(2)}, u32[]{:S(2)}) async-start(bf16[64,32,128]{2,1,0:T(8,128)(2,1)} %shard_map.70), calls=%async_computation.2 | async-start | bytes 1048576 | tf_op jit(solution)/shard_map/all_to_all | solution.py:273
  99.0 12.8 %all-to-all-done.2.in_ref = bf16[64,32,128]{2,1,0:T(8,128)(2,1)S(1)} async-done(((bf16[64,32,128]{2,1,0:T(8,128)(2,1)}), bf16[64,32,128]{2,1,0:T(8,128)(2,1)S(1)}, u32[]{:S(2)}, u32[]{:S(2)}) %all-to-all-start.2) | async-done | bytes 524320 | tf_op jit(solution)/shard_map/all_to_all | solution.py:273
  111.8 1.0 shard_map.71
  (3 shorter events, 0.0 us)
Async XLA Ops:
  3.4 11.0 %copy-start.2 = (bf16[48,128]{1,0:T(8,128)(2,1)S(1)}, bf16[48,128]{1,0:T(8,128)(2,1)}, u32[]{:S(2)}) copy-start(bf16[48,128]{1,0:T(8,128)(2,1)} %get-tuple-element.9) | copy-start | bytes 36868
  3.4 14.3 %copy-start = (bf16[48,128]{1,0:T(8,128)(2,1)S(1)}, bf16[48,128]{1,0:T(8,128)(2,1)}, u32[]{:S(2)}) copy-start(bf16[48,128]{1,0:T(8,128)(2,1)} %get-tuple-element.8) | copy-start | bytes 36868
  3.4 49.0 %all-to-all-start = ((bf16[64,48,128]{2,1,0:T(8,128)(2,1)}), bf16[64,48,128]{2,1,0:T(8,128)(2,1)S(1)}, u32[]{:S(2)}, u32[]{:S(2)}) async-start(bf16[64,48,128]{2,1,0:T(8,128)(2,1)} %get-tuple-element.7), calls=%async_computation | async-start | bytes 1572864 | tf_op jit(solution)/shard_map/all_to_all | solution.py:273
  14.4 3.3 %collective-permute-start = (bf16[48,128]{1,0:T(8,128)(2,1)S(1)}, bf16[48,128]{1,0:T(8,128)(2,1)S(1)}, u32[]{:S(2)}, u32[]{:S(2)}) collective-permute-start(bf16[48,128]{1,0:T(8,128)(2,1)S(1)} %copy-done.2), channel_id=1, source_target_pairs={{0,16},{16,0},{1,17},{17,1},{2,18},{18,2},{3,19},{19,3},{4,20},{20... | collective-permute-start | bytes 36872 | tf_op jit(solution)/shard_map/ppermute | solution.py:299
  57.7 25.6 %all-to-all-start.1 = ((f32[8,72,128]{2,1,0:T(8,128)}), f32[8,72,128]{2,1,0:T(8,128)S(1)}, u32[]{:S(2)}, u32[]{:S(2)}) async-start(f32[8,72,128]{2,1,0:T(8,128)} %shard_map.69), calls=%async_computation.1 | async-start | bytes 589824 | tf_op jit(solution)/shard_map/all_to_all | solution.py:273
  64.2 0.7 copy-start.1
  87.2 24.6 %all-to-all-start.2 = ((bf16[64,32,128]{2,1,0:T(8,128)(2,1)}), bf16[64,32,128]{2,1,0:T(8,128)(2,1)S(1)}, u32[]{:S(2)}, u32[]{:S(2)}) async-start(bf16[64,32,128]{2,1,0:T(8,128)(2,1)} %shard_map.70), calls=%async_computation.2 | async-start | bytes 1048576 | tf_op jit(solution)/shard_map/all_to_all | solution.py:273

commit v2 on v1

--- a/solution.py
+++ b/solution.py
@@ -125,7 +125,7 @@
         )
 
     start = jnp.full((8, queries), -1e30, F32)
-    tops = lax.fori_loop(0, steps, measure, (start, start), unroll=True)
+    tops = lax.fori_loop(0, steps, measure, (start, start), unroll=2)
     tops = [jnp.max(top, axis=0, keepdims=True) * scale for top, scale in zip(tops, scales)]
 
     def gather(index, state):
@@ -159,7 +159,7 @@
 
     none = jnp.zeros((8, queries), F32)
     state = lax.fori_loop(
-        0, steps, gather, (none, none, jnp.zeros((LANES, queries), F32)), unroll=True
+        0, steps, gather, (none, none, jnp.zeros((LANES, queries), F32)), unroll=2
     )
     lines, columns = [], []
     for kind in range(2):
@@ -176,7 +176,8 @@
 
 
 def grads_kernel(
-    chunk, near_ref, logs_ref, weights_ref, own_ref, keys_ref, rows_ref, key_ref, span_ref
+    chunk, near_ref, logs_ref, weights_ref, own_ref, keys_ref, rows_ref, key_ref, own_out_ref,
+    span_ref, mean_ref,
 ):
     deep = logs_ref.shape[1] - 8
     logs = logs_ref[:, deep:, :]
@@ -188,18 +189,17 @@
     weights = weights_ref[...]
     teach_q, left_q, right_q = queries_of(near_ref, rows_ref)
     span_ref[0], span_ref[1], span_ref[2] = teach_q, left_q, right_q
-    own = key_ref.shape[1] // 2
+    own = key_ref.shape[1]
 
     means = logs_ref[:, :deep, :]
     each = jnp.where(low_lanes(3), means[:, :, SH : SH + 1], means[:, :, HALF + SH : HALF + SH + 1])
     share = jnp.exp2(each - jnp.max(each, axis=0, keepdims=True))
     mean = jnp.sum(share * means, axis=0) / jnp.sum(share, axis=0)
     mean = (turn(mean) - mean) * own_ref[...] * (1.0 / math.sqrt(SH))
-    rough = mean.astype(BF16).astype(F32)
-    mean = jnp.where(low_lanes(2), rough, turn(mean - rough)).astype(BF16)
-    for head in range(key_ref.shape[0]):
-        start = head % (deep // own) * own
-        key_ref[head, own:, :] = mean[start : start + own]
+    mean_ref[...] = mean.reshape(mean_ref.shape)
+    spot = near_ref[0] * CORES + near_ref[1]
+    for step_to in range(NEAR * CORES):
+        own_out_ref[step_to] = mean_ref[spot ^ step_to]
 
     def grad(teach_score, stud_score):
         teach = jnp.exp2(teach_score * (LOG2E / math.sqrt(TH)) - teach_log)
@@ -213,28 +213,35 @@
         mix = jnp.dot(left, span_ref[1], preferred_element_type=F32)
         mix = mix + jnp.dot(right, span_ref[2], preferred_element_type=F32)
         mix = (mix * (1.0 / math.sqrt(SH))).astype(key_ref.dtype)
-        key_ref[pl.ds(index * chunk, chunk), :own, :] = mix.reshape(chunk, own, LANES)
+        key_ref[pl.ds(index * chunk, chunk)] = mix.reshape(chunk, own, LANES)
         return 0
 
-    lax.fori_loop(0, keys_ref.shape[0] // chunk, step, 0, unroll=True)
-
-
-def unpack(tp_ref, in_ref, context_ref, span_ref):
-    half = in_ref.shape[1] // 2
+    lax.fori_loop(0, keys_ref.shape[0] // chunk, step, 0, unroll=2)
+
+
+def unpack_keys(in_ref, out_ref):
+    half = in_ref.shape[1]
     group = 16
     for start in range(0, in_ref.shape[0], group):
         for side in range(2):
             parts = [
-                in_ref[head, :half, side * HALF : side * HALF + SH].astype(F32)
+                in_ref[head, :, side * HALF : side * HALF + SH].astype(F32)
                 for head in range(start, start + group)
             ]
-            context_ref[side * half : (side + 1) * half, start * SH : (start + group) * SH] = (
+            out_ref[side * half : (side + 1) * half, start * SH : (start + group) * SH] = (
                 jnp.concatenate(parts, axis=1)
             )
-    near = NEAR * CORES
-    rows = in_ref[pl.ds(tp_ref[0] * near, near), half:, :].astype(F32)
-    rows = rows + turn(rows)
-    span_ref[...] = jnp.concatenate([rows[head, :, :SH] for head in range(near)], axis=1)
+
+
+def unpack_rows(near_ref, mine_ref, along_ref, across_ref, out_ref, part_ref):
+    spot = near_ref[0] * CORES + near_ref[1]
+    part_ref[spot] = mine_ref[0]
+    part_ref[spot ^ 2] = along_ref[0]
+    part_ref[spot ^ 1] = across_ref[0]
+    part_ref[spot ^ 3] = across_ref[1]
+    out_ref[...] = jnp.concatenate(
+        [part_ref[head, :, :SH] for head in range(part_ref.shape[0])], axis=1
+    )
 
 
 def call(body, shapes, scratch=(), smem=0, raw=0, raw_out=0, flops=0, room=48):
@@ -272,7 +279,8 @@
     def trade(array, axes):
         return lax.all_to_all(array, axes, split_axis=0, concat_axis=0, tiled=True)
 
-    core, spot = lax.axis_index("core"), lax.axis_index("near").astype(jnp.int32).reshape(1)
+    core = lax.axis_index("core").astype(jnp.int32)
+    spot = jnp.stack([lax.axis_index("near").astype(jnp.int32), core])
     piece = shape(((NEAR + 1) * rows_own, LANES), BF16)
     keys, kept, given = call(
         pack,
@@ -290,7 +298,7 @@
         raw_out=1,
         room=62,
     )(
-        (spot[0] ^ core).astype(jnp.int32).reshape(1),
+        (spot[:1] ^ core),
         teacher_span,
         teacher_context,
         student_span,
@@ -327,17 +335,24 @@
     weights = math.sqrt(tokens_all) * query_weights
     own = lax.dynamic_slice(weights, (lax.axis_index("group") * deep,), (deep,))
     own = jnp.broadcast_to(own[:, None], (deep, LANES))
-    parts = call(
+    parts, mine = call(
         functools.partial(grads_kernel, 8),
-        shape((heads, 2 * half, LANES), BF16),
-        scratch=[spans],
+        (shape((heads, half, LANES), BF16), shape((near, rows_own, LANES), F32)),
+        scratch=[spans, pltpu.VMEM((near, rows_own, LANES), F32)],
         smem=1,
         flops=2**30,
     )(spot, logs, weights.reshape(1, queries), own, keys, rows)
     parts = trade(parts, ("tp", "near", "core"))
-    grad_context, grad_span = call(
-        unpack, (shape((tokens_own, heads * SH), F32), shape((rows_own, near * SH), F32)), smem=1
-    )(lax.axis_index("tp").astype(jnp.int32).reshape(1), parts)
+    flip = lambda array, axis: lax.ppermute(array, axis, [(0, 1), (1, 0)])
+    along = flip(mine[CORES:], "near")
+    across = flip(jnp.stack([mine[1], along[1]]), "core")
+    grad_span = call(
+        unpack_rows,
+        shape((rows_own, near * SH), F32),
+        scratch=[pltpu.VMEM((near, rows_own, LANES), F32)],
+        smem=1,
+    )(spot, mine, along, across)
+    grad_context = call(unpack_keys, shape((tokens_own, heads * SH), F32))(parts)
     return (grad_span, grad_context)
 
 

time: 113 us -> 113 us (level)
  waiting for transfers between devices: 32 us -> 21.9 us
  starting transfers between devices: 31.7 us -> 37.8 us
  Pallas kernels: 12.8 us -> 16.7 us
    all_to_all x3, waiting for transfers between devices: 31.2 us -> 18.5 us  [trade(): return lax.all_to_all(array, axes, split_axis=0, concat_axis=0, tiled=True)]
    ppermute x0 -> x2, starting transfers between devices: none -> 6.13 us  [on_device(): flip = lambda array, axis: lax.ppermute(array, axis, [(0, 1), (1, 0)])]
    pallas_call x4 -> x5, Pallas kernels: 12.8 us -> 16.7 us  [run(): pl.pallas_call(body, out_shape=shapes, in_specs=specs((smem, raw, len(arg...]
    ppermute x0 -> x2, waiting for transfers between devices: none -> 2.65 us  [on_device(): flip = lambda array, axis: lax.ppermute(array, axis, [(0, 1), (1, 0)])]
  transfers between devices with their start and end apart: 4 -> 6, of which waited for: 3 -> 5; matrix products, arithmetic and copies ran while one was open for 0% -> 0% of each run, Pallas kernels for 0% -> 1%
where the time goes in v2:
time: 113 us
  starting transfers between devices  37.8 us (33%)
  blocking collectives  34.7 us (31%)
  waiting for transfers between devices  21.9 us (19%)
  Pallas kernels  16.7 us (15%)
    all_gather x1, blocking collectives, on_device(): lax.all_gather(shard, ('group', 'near', 'core'), axis=0, tiled=True, axis...  34.7 us
    all_to_all x3, starting transfers between devices, trade(): return lax.all_to_all(array, axes, split_axis=0, concat_axis=0, tiled=True)  29.2 us
    all_to_all x3, waiting for transfers between devices, trade(): return lax.all_to_all(array, axes, split_axis=0, concat_axis=0, tiled=True)  18.5 us
    pallas_call x5, Pallas kernels, run(): pl.pallas_call(body, out_shape=shapes, in_specs=specs((smem, raw, len(arg...  16.7 us
    ppermute x2, starting transfers between devices, on_device(): flip = lambda array, axis: lax.ppermute(array, axis, [(0, 1), (1, 0)])  6.13 us
    ppermute x2, waiting for transfers between devices, on_device(): flip = lambda array, axis: lax.ppermute(array, axis, [(0, 1), (1, 0)])  2.65 us
    ppermute x1, starting transfers between devices, on_device(): other = lax.ppermute(given, 'core', [(0, 1), (1, 0)])  2.48 us
  transfers between devices with their start and end apart: 6, of which 5 were waited for; matrix products, arithmetic and copies ran while one was open for 0% of the time, Pallas kernels for 1%

profile of v2, /device:TPU:1, one launch (start us, length us, event | category | flops | bytes accessed | tf_op | source)
XLA Modules:
  0.0 112.8 jit_solution(5093520817669532387)
XLA Ops:
  0.6 2.8 %shard_map.68 = (bf16[64,48,128]{2,1,0:T(8,128)(2,1)}, bf16[48,128]{1,0:T(8,128)(2,1)}, bf16[48,128]{1,0:T(8,128)(2,1)}) custom-call(s32[1]{0:T(128)S(6)} %xor.4.side_ref, bf16[16,512]{1,0:T(8,128)(2,1)} %tq_hbm.1, bf16[32,8192]{1,0:T(8,128)(2,1)} %tk_hbm.1, bf16[16,160]{1,0:T(8,128)(2,1)} %sq_hbm.1, bf16[32,2560]{1,0:T(8,128)(2,1)} %sk_hbm.1), custom_call_target="tpu_custom_call" | custom-call | bytes 709636 | tf_op jit(solution)/shard_map/pallas_call | solution.py:257
  3.4 0.0 copy-start.2
  3.4 0.0 copy-start
  3.4 11.0 %all-to-all-start = ((bf16[64,48,128]{2,1,0:T(8,128)(2,1)}), bf16[64,48,128]{2,1,0:T(8,128)(2,1)S(1)}, u32[]{:S(2)}, u32[]{:S(2)}) async-start(bf16[64,48,128]{2,1,0:T(8,128)(2,1)} %get-tuple-element.7), calls=%async_computation | async-start | bytes 1572864 | tf_op jit(solution)/shard_map/all_to_all | solution.py:280
  14.4 0.0 copy-done.2
  14.4 2.5 %collective-permute-start = (bf16[48,128]{1,0:T(8,128)(2,1)S(1)}, bf16[48,128]{1,0:T(8,128)(2,1)S(1)}, u32[]{:S(2)}, u32[]{:S(2)}) collective-permute-start(bf16[48,128]{1,0:T(8,128)(2,1)S(1)} %copy-done.2), channel_id=1, source_target_pairs={{0,16},{16,0},{1,17},{17,1},{2,18},{18,2},{3,19},{19,3},{4,20},{20... | collective-permute-start | bytes 36872 | tf_op jit(solution)/shard_map/ppermute | solution.py:307
  16.9 0.1 pad_add_fusion.near_ref
  17.0 0.7 collective-permute-done
  17.7 0.0 copy-done
  17.7 34.7 %all_gather.3.rows_ref = bf16[16,96,128]{2,1,0:T(8,128)(2,1)S(1)} all-gather(bf16[1,96,128]{2,1,0:T(8,128)(2,1)S(1)} %bitcast.7), channel_id=1, replica_groups={{0,48,64,112,128,176,192,240,256,304,320,368,384,432,448,496},{16,32,80..., dimensions={0}, use_global_device_ids=true | all-gather | bytes 417792 | tf_op jit(solution)/shard_map/all_gather | solution.py:314
  52.4 0.0 all-to-all-done.keys_ref
  52.4 6.8 %shard_map.69 = f32[8,72,128]{2,1,0:T(8,128)} custom-call(s32[2]{0:T(128)S(1)} %pad_add_fusion.near_ref, bf16[64,48,128]{2,1,0:T(8,128)(2,1)S(1)} %all-to-all-done.keys_ref, bf16[16,96,128]{2,1,0:T(8,128)(2,1)S(1)} %all_gather.3.rows_ref), custom_call_target="tpu_custom_call" | custom-call | flops 2147483648 | bytes 1179656 | tf_op jit(solution)/shard_map/pallas_call | solution.py:257
  59.3 6.5 %all-to-all-start.1 = ((f32[8,72,128]{2,1,0:T(8,128)}), f32[8,72,128]{2,1,0:T(8,128)S(1)}, u32[]{:S(2)}, u32[]{:S(2)}) async-start(f32[8,72,128]{2,1,0:T(8,128)} %shard_map.69), calls=%async_computation.1 | async-start | bytes 589824 | tf_op jit(solution)/shard_map/all_to_all | solution.py:280
  65.7 0.0 copy-start.1
  65.8 0.7 copy-done.1
  66.4 0.1 dynamic_slice.3
  66.5 18.4 %all-to-all-done.1.logs_ref = f32[8,72,128]{2,1,0:T(8,128)S(1)} async-done(((f32[8,72,128]{2,1,0:T(8,128)}), f32[8,72,128]{2,1,0:T(8,128)S(1)}, u32[]{:S(2)}, u32[]{:S(2)}) %all-to-all-start.1) | async-done | bytes 294944 | tf_op jit(solution)/shard_map/all_to_all | solution.py:280
  84.9 0.1 broadcast_in_dim.2.own_ref
  85.0 4.9 %shard_map.70 = (bf16[64,16,128]{2,1,0:T(8,128)(2,1)}, f32[4,16,128]{2,1,0:T(8,128)S(1)}) custom-call(s32[2]{0:T(128)S(1)} %pad_add_fusion.near_ref, f32[8,72,128]{2,1,0:T(8,128)S(1)} %all-to-all-done.1.logs_ref, f32[1,512]{1,0:T(1,128)S(1)} %bitcast.6, f32[64,128]{1,0:T(8,128)S(1)} %broadcast_in_dim.2.own_ref, ...), custom_call_target="tpu_custom_call" | custom-call | flops 1073741824 | bytes 1509384 | tf_op jit(solution)/shard_map/pallas_call | solution.py:257
  89.9 11.8 %all-to-all-start.2 = ((bf16[64,16,128]{2,1,0:T(8,128)(2,1)}), bf16[64,16,128]{2,1,0:T(8,128)(2,1)S(1)}, u32[]{:S(2)}, u32[]{:S(2)}) async-start(bf16[64,16,128]{2,1,0:T(8,128)(2,1)} %get-tuple-element.11), calls=%async_computation.2 | async-start | bytes 524288 | tf_op jit(solution)/shard_map/all_to_all | solution.py:280
  101.7 3.3 %collective-permute-start.1 = (f32[2,16,128]{2,1,0:T(8,128)S(1)}, f32[2,16,128]{2,1,0:T(8,128)S(1)}, u32[]{:S(2)}, u32[]{:S(2)}) collective-permute-start(f32[2,16,128]{2,1,0:T(8,128)S(1)} %slice.9), channel_id=1, source_target_pairs={{0,32},{32,0},{1,33},{33,1},{2,34},{34,2},{3,35},{35,3},{4,36},{36... | collective-permute-start | bytes 49160 | tf_op jit(solution)/shard_map/ppermute | solution.py:346
  105.0 1.8 %collective-permute-done.1.along_ref = f32[2,16,128]{2,1,0:T(8,128)S(1)} collective-permute-done((f32[2,16,128]{2,1,0:T(8,128)S(1)}, f32[2,16,128]{2,1,0:T(8,128)S(1)}, u32[]{:S(2)}, u32[]{:S(2)}) %collective-permute-start.1) | collective-permute-done | bytes 16416 | tf_op jit(solution)/shard_map/ppermute | solution.py:346
  106.9 2.8 %collective-permute-start.2 = (f32[2,16,128]{2,1,0:T(8,128)S(1)}, f32[2,16,128]{2,1,0:T(8,128)S(1)}, u32[]{:S(2)}, u32[]{:S(2)}) collective-permute-start(f32[2,16,128]{2,1,0:T(8,128)S(1)} %pad_maximum_fusion), channel_id=1, source_target_pairs={{0,16},{16,0},{1,17},{17,1},{2,18},{18,2},{3,19},{19,3},{4,20},{20... | collective-permute-start | bytes 49160 | tf_op jit(solution)/shard_map/ppermute | solution.py:346
  109.7 0.8 collective-permute-done.2.across_ref
  110.5 1.2 %shard_map.71 = f32[16,160]{1,0:T(8,128)} custom-call(s32[2]{0:T(128)S(1)} %pad_add_fusion.near_ref, f32[4,16,128]{2,1,0:T(8,128)S(1)} %get-tuple-element.10.mine_ref, f32[2,16,128]{2,1,0:T(8,128)S(1)} %collective-permute-done.1.along_ref, f32[2,16,128]{2,1,0:T(8,128)S(1)} %collective-permute-done.2.across_ref), custom_call_target="tpu_custom_call" | custom-call | bytes 65544 | tf_op jit(solution)/shard_map/pallas_call | solution.py:257
  111.8 0.1 all-to-all-done.2.in_ref
  111.9 0.9 shard_map.72
  (7 shorter events, 0.0 us)
Async XLA Ops:
  3.4 11.0 %copy-start.2 = (bf16[48,128]{1,0:T(8,128)(2,1)S(1)}, bf16[48,128]{1,0:T(8,128)(2,1)}, u32[]{:S(2)}) copy-start(bf16[48,128]{1,0:T(8,128)(2,1)} %get-tuple-element.9) | copy-start | bytes 36868
  3.4 14.3 %copy-start = (bf16[48,128]{1,0:T(8,128)(2,1)S(1)}, bf16[48,128]{1,0:T(8,128)(2,1)}, u32[]{:S(2)}) copy-start(bf16[48,128]{1,0:T(8,128)(2,1)} %get-tuple-element.8) | copy-start | bytes 36868
  3.4 49.0 %all-to-all-start = ((bf16[64,48,128]{2,1,0:T(8,128)(2,1)}), bf16[64,48,128]{2,1,0:T(8,128)(2,1)S(1)}, u32[]{:S(2)}, u32[]{:S(2)}) async-start(bf16[64,48,128]{2,1,0:T(8,128)(2,1)} %get-tuple-element.7), calls=%async_computation | async-start | bytes 1572864 | tf_op jit(solution)/shard_map/all_to_all | solution.py:280
  14.4 3.3 %collective-permute-start = (bf16[48,128]{1,0:T(8,128)(2,1)S(1)}, bf16[48,128]{1,0:T(8,128)(2,1)S(1)}, u32[]{:S(2)}, u32[]{:S(2)}) collective-permute-start(bf16[48,128]{1,0:T(8,128)(2,1)S(1)} %copy-done.2), channel_id=1, source_target_pairs={{0,16},{16,0},{1,17},{17,1},{2,18},{18,2},{3,19},{19,3},{4,20},{20... | collective-permute-start | bytes 36872 | tf_op jit(solution)/shard_map/ppermute | solution.py:307
  59.3 25.7 %all-to-all-start.1 = ((f32[8,72,128]{2,1,0:T(8,128)}), f32[8,72,128]{2,1,0:T(8,128)S(1)}, u32[]{:S(2)}, u32[]{:S(2)}) async-start(f32[8,72,128]{2,1,0:T(8,128)} %shard_map.69), calls=%async_computation.1 | async-start | bytes 589824 | tf_op jit(solution)/shard_map/all_to_all | solution.py:280
  65.7 0.7 copy-start.1
  89.9 21.9 %all-to-all-start.2 = ((bf16[64,16,128]{2,1,0:T(8,128)(2,1)}), bf16[64,16,128]{2,1,0:T(8,128)(2,1)S(1)}, u32[]{:S(2)}, u32[]{:S(2)}) async-start(bf16[64,16,128]{2,1,0:T(8,128)(2,1)} %get-tuple-element.11), calls=%async_computation.2 | async-start | bytes 524288 | tf_op jit(solution)/shard_map/all_to_all | solution.py:280
  101.7 5.1 %collective-permute-start.1 = (f32[2,16,128]{2,1,0:T(8,128)S(1)}, f32[2,16,128]{2,1,0:T(8,128)S(1)}, u32[]{:S(2)}, u32[]{:S(2)}) collective-permute-start(f32[2,16,128]{2,1,0:T(8,128)S(1)} %slice.9), channel_id=1, source_target_pairs={{0,32},{32,0},{1,33},{33,1},{2,34},{34,2},{3,35},{35,3},{4,36},{36... | collective-permute-start | bytes 49160 | tf_op jit(solution)/shard_map/ppermute | solution.py:346
  106.9 3.7 %collective-permute-start.2 = (f32[2,16,128]{2,1,0:T(8,128)S(1)}, f32[2,16,128]{2,1,0:T(8,128)S(1)}, u32[]{:S(2)}, u32[]{:S(2)}) collective-permute-start(f32[2,16,128]{2,1,0:T(8,128)S(1)} %pad_maximum_fusion), channel_id=1, source_target_pairs={{0,16},{16,0},{1,17},{17,1},{2,18},{18,2},{3,19},{19,3},{4,20},{20... | collective-permute-start | bytes 49160 | tf_op jit(solution)/shard_map/ppermute | solution.py:346

commit v3 on v2

--- a/solution.py
+++ b/solution.py
@@ -125,7 +125,7 @@
         )
 
     start = jnp.full((8, queries), -1e30, F32)
-    tops = lax.fori_loop(0, steps, measure, (start, start), unroll=2)
+    tops = lax.fori_loop(0, steps, measure, (start, start), unroll=True)
     tops = [jnp.max(top, axis=0, keepdims=True) * scale for top, scale in zip(tops, scales)]
 
     def gather(index, state):
@@ -159,7 +159,7 @@
 
     none = jnp.zeros((8, queries), F32)
     state = lax.fori_loop(
-        0, steps, gather, (none, none, jnp.zeros((LANES, queries), F32)), unroll=2
+        0, steps, gather, (none, none, jnp.zeros((LANES, queries), F32)), unroll=True
     )
     lines, columns = [], []
     for kind in range(2):
@@ -176,8 +176,8 @@
 
 
 def grads_kernel(
-    chunk, near_ref, logs_ref, weights_ref, own_ref, keys_ref, rows_ref, key_ref, own_out_ref,
-    span_ref, mean_ref,
+    chunk, near_ref, core_ref, logs_ref, weights_ref, own_ref, keys_ref, span_ref, key_ref,
+    own_out_ref, mean_ref,
 ):
     deep = logs_ref.shape[1] - 8
     logs = logs_ref[:, deep:, :]
@@ -187,8 +187,6 @@
     flat = lambda rows: jnp.concatenate([rows[k : k + 1] for k in range(lines)], axis=1)
     teach_log, stud_log = flat(logs[:lines]), flat(logs[lines:])
     weights = weights_ref[...]
-    teach_q, left_q, right_q = queries_of(near_ref, rows_ref)
-    span_ref[0], span_ref[1], span_ref[2] = teach_q, left_q, right_q
     own = key_ref.shape[1]
 
     means = logs_ref[:, :deep, :]
@@ -197,7 +195,7 @@
     mean = jnp.sum(share * means, axis=0) / jnp.sum(share, axis=0)
     mean = (turn(mean) - mean) * own_ref[...] * (1.0 / math.sqrt(SH))
     mean_ref[...] = mean.reshape(mean_ref.shape)
-    spot = near_ref[0] * CORES + near_ref[1]
+    spot = near_ref[0] * CORES + core_ref[0]
     for step_to in range(NEAR * CORES):
         own_out_ref[step_to] = mean_ref[spot ^ step_to]
 
@@ -216,7 +214,7 @@
         key_ref[pl.ds(index * chunk, chunk)] = mix.reshape(chunk, own, LANES)
         return 0
 
-    lax.fori_loop(0, keys_ref.shape[0] // chunk, step, 0, unroll=2)
+    lax.fori_loop(0, keys_ref.shape[0] // chunk, step, 0, unroll=True)
 
 
 def unpack_keys(in_ref, out_ref):
@@ -233,8 +231,8 @@
             )
 
 
-def unpack_rows(near_ref, mine_ref, along_ref, across_ref, out_ref, part_ref):
-    spot = near_ref[0] * CORES + near_ref[1]
+def unpack_rows(near_ref, core_ref, mine_ref, along_ref, across_ref, out_ref, part_ref):
+    spot = near_ref[0] * CORES + core_ref[0]
     part_ref[spot] = mine_ref[0]
     part_ref[spot ^ 2] = along_ref[0]
     part_ref[spot ^ 1] = across_ref[0]
@@ -280,7 +278,8 @@
         return lax.all_to_all(array, axes, split_axis=0, concat_axis=0, tiled=True)
 
     core = lax.axis_index("core").astype(jnp.int32)
-    spot = jnp.stack([lax.axis_index("near").astype(jnp.int32), core])
+    side = core.reshape(1)
+    spot = lax.axis_index("near").astype(jnp.int32).reshape(1)
     piece = shape(((NEAR + 1) * rows_own, LANES), BF16)
     keys, kept, given = call(
         pack,
@@ -298,7 +297,7 @@
         raw_out=1,
         room=62,
     )(
-        (spot[:1] ^ core),
+        spot ^ side,
         teacher_span,
         teacher_context,
         student_span,
@@ -321,12 +320,11 @@
         ],
     )
 
-    spans = pltpu.VMEM((3, queries, LANES), BF16)
     deep = queries // groups
-    logs = call(
+    logs, spans = call(
         functools.partial(totals_kernel, 8),
-        shape((groups, deep + 8, LANES), F32),
-        scratch=[spans, pltpu.VMEM((4, heads * half, queries), F32)],
+        (shape((groups, deep + 8, LANES), F32), shape((3, queries, LANES), BF16)),
+        scratch=[pltpu.VMEM((4, heads * half, queries), F32)],
         smem=1,
         flops=2**31,
     )(spot, keys, rows)
@@ -338,10 +336,10 @@
     parts, mine = call(
         functools.partial(grads_kernel, 8),
         (shape((heads, half, LANES), BF16), shape((near, rows_own, LANES), F32)),
-        scratch=[spans, pltpu.VMEM((near, rows_own, LANES), F32)],
-        smem=1,
+        scratch=[pltpu.VMEM((near, rows_own, LANES), F32)],
+        smem=2,
         flops=2**30,
-    )(spot, logs, weights.reshape(1, queries), own, keys, rows)
+    )(spot, side, logs, weights.reshape(1, queries), own, keys, spans)
     parts = trade(parts, ("tp", "near", "core"))
     flip = lambda array, axis: lax.ppermute(array, axis, [(0, 1), (1, 0)])
     along = flip(mine[CORES:], "near")
@@ -350,8 +348,8 @@
         unpack_rows,
         shape((rows_own, near * SH), F32),
         scratch=[pltpu.VMEM((near, rows_own, LANES), F32)],
-        smem=1,
-    )(spot, mine, along, across)
+        smem=2,
+    )(spot, side, mine, along, across)
     grad_context = call(unpack_keys, shape((tokens_own, heads * SH), F32))(parts)
     return (grad_span, grad_context)
 

time: 113 us -> 110 us (0.973)
  Pallas kernels: 16.7 us -> 13.3 us
    pallas_call x5, Pallas kernels: 16.7 us -> 13.3 us  [run(): pl.pallas_call(body, out_shape=shapes, in_specs=specs((smem, raw, len(arg...]
where the time goes in v3:
time: 110 us
  starting transfers between devices  37.9 us (34%)
  blocking collectives  34.7 us (32%)
  waiting for transfers between devices  22.5 us (20%)
  Pallas kernels  13.3 us (12%)
    all_gather x1, blocking collectives, on_device(): lax.all_gather(shard, ('group', 'near', 'core'), axis=0, tiled=True, axis...  34.7 us
    all_to_all x3, starting transfers between devices, trade(): return lax.all_to_all(array, axes, split_axis=0, concat_axis=0, tiled=True)  29.3 us
    all_to_all x3, waiting for transfers between devices, trade(): return lax.all_to_all(array, axes, split_axis=0, concat_axis=0, tiled=True)  19 us
    pallas_call x5, Pallas kernels, run(): pl.pallas_call(body, out_shape=shapes, in_specs=specs((smem, raw, len(arg...  13.3 us
    ppermute x2, starting transfers between devices, on_device(): flip = lambda array, axis: lax.ppermute(array, axis, [(0, 1), (1, 0)])  6.13 us
    ppermute x2, waiting for transfers between devices, on_device(): flip = lambda array, axis: lax.ppermute(array, axis, [(0, 1), (1, 0)])  2.65 us
    ppermute x1, starting transfers between devices, on_device(): other = lax.ppermute(given, 'core', [(0, 1), (1, 0)])  2.48 us
  transfers between devices with their start and end apart: 6, of which 5 were waited for; matrix products, arithmetic and copies ran while one was open for 0% of the time, Pallas kernels for 1%

profile of v3, /device:TPU:1, one launch (start us, length us, event | category | flops | bytes accessed | tf_op | source)
XLA Modules:
  0.0 109.9 jit_solution(2560364166418262630)
XLA Ops:
  0.6 2.8 %shard_map.68 = (bf16[64,48,128]{2,1,0:T(8,128)(2,1)}, bf16[48,128]{1,0:T(8,128)(2,1)}, bf16[48,128]{1,0:T(8,128)(2,1)}) custom-call(s32[1]{0:T(128)S(6)} %xor.3.side_ref, bf16[16,512]{1,0:T(8,128)(2,1)} %tq_hbm.1, bf16[32,8192]{1,0:T(8,128)(2,1)} %tk_hbm.1, bf16[16,160]{1,0:T(8,128)(2,1)} %sq_hbm.1, bf16[32,2560]{1,0:T(8,128)(2,1)} %sk_hbm.1), custom_call_target="tpu_custom_call" | custom-call | bytes 709636 | tf_op jit(solution)/shard_map/pallas_call | solution.py:255
  3.4 0.0 copy-start.2
  3.4 0.0 copy-start
  3.5 11.0 %all-to-all-start = ((bf16[64,48,128]{2,1,0:T(8,128)(2,1)}), bf16[64,48,128]{2,1,0:T(8,128)(2,1)S(1)}, u32[]{:S(2)}, u32[]{:S(2)}) async-start(bf16[64,48,128]{2,1,0:T(8,128)(2,1)} %get-tuple-element.9), calls=%async_computation | async-start | bytes 1572864 | tf_op jit(solution)/shard_map/all_to_all | solution.py:278
  14.4 0.0 copy-done.2
  14.4 2.5 %collective-permute-start = (bf16[48,128]{1,0:T(8,128)(2,1)S(1)}, bf16[48,128]{1,0:T(8,128)(2,1)S(1)}, u32[]{:S(2)}, u32[]{:S(2)}) collective-permute-start(bf16[48,128]{1,0:T(8,128)(2,1)S(1)} %copy-done.2), channel_id=1, source_target_pairs={{0,16},{16,0},{1,17},{17,1},{2,18},{18,2},{3,19},{19,3},{4,20},{20... | collective-permute-start | bytes 36872 | tf_op jit(solution)/shard_map/ppermute | solution.py:306
  16.9 0.8 collective-permute-done
  17.7 0.0 copy-done
  17.8 34.7 %all_gather.3.rows_ref = bf16[16,96,128]{2,1,0:T(8,128)(2,1)S(1)} all-gather(bf16[1,96,128]{2,1,0:T(8,128)(2,1)S(1)} %bitcast.7), channel_id=1, replica_groups={{0,48,64,112,128,176,192,240,256,304,320,368,384,432,448,496},{16,32,80..., dimensions={0}, use_global_device_ids=true | all-gather | bytes 417792 | tf_op jit(solution)/shard_map/all_gather | solution.py:313
  52.4 0.0 all-to-all-done.keys_ref
  52.5 5.3 %shard_map.69 = (f32[8,72,128]{2,1,0:T(8,128)}, bf16[3,512,128]{2,1,0:T(8,128)(2,1)S(1)}) custom-call(s32[1]{0:T(128)} %bitcast.near_ref, bf16[64,48,128]{2,1,0:T(8,128)(2,1)S(1)} %all-to-all-done.keys_ref, bf16[16,96,128]{2,1,0:T(8,128)(2,1)S(1)} %all_gather.3.rows_ref), custom_call_target="tpu_custom_call" | custom-call | flops 2147483648 | bytes 1179652 | tf_op jit(solution)/shard_map/pallas_call | solution.py:255
  57.8 6.5 %all-to-all-start.1 = ((f32[8,72,128]{2,1,0:T(8,128)}), f32[8,72,128]{2,1,0:T(8,128)S(1)}, u32[]{:S(2)}, u32[]{:S(2)}) async-start(f32[8,72,128]{2,1,0:T(8,128)} %get-tuple-element.12), calls=%async_computation.1 | async-start | bytes 589824 | tf_op jit(solution)/shard_map/all_to_all | solution.py:278
  64.3 0.0 copy-start.1
  64.3 0.7 copy-done.1
  64.9 0.1 dynamic_slice.3
  65.0 18.4 %all-to-all-done.1.logs_ref = f32[8,72,128]{2,1,0:T(8,128)S(1)} async-done(((f32[8,72,128]{2,1,0:T(8,128)}), f32[8,72,128]{2,1,0:T(8,128)S(1)}, u32[]{:S(2)}, u32[]{:S(2)}) %all-to-all-start.1) | async-done | bytes 294944 | tf_op jit(solution)/shard_map/all_to_all | solution.py:278
  83.4 0.1 broadcast_in_dim.2.own_ref
  83.5 3.5 %shard_map.70 = (bf16[64,16,128]{2,1,0:T(8,128)(2,1)}, f32[4,16,128]{2,1,0:T(8,128)S(1)}) custom-call(s32[1]{0:T(128)} %bitcast.near_ref, s32[1]{0:T(128)} %bitcast.1.core_ref, f32[8,72,128]{2,1,0:T(8,128)S(1)} %all-to-all-done.1.logs_ref, f32[1,512]{1,0:T(1,128)S(1)} %bitcast.6, f32[64,128]{1,0:T(8,128)S(1)} %broadcast_in_dim.2.own_ref, ...), custom_call_target="tpu_custom_call" | custom-call | flops 1073741824 | bytes 1509384 | tf_op jit(solution)/shard_map/pallas_call | solution.py:255
  87.0 11.8 %all-to-all-start.2 = ((bf16[64,16,128]{2,1,0:T(8,128)(2,1)}), bf16[64,16,128]{2,1,0:T(8,128)(2,1)S(1)}, u32[]{:S(2)}, u32[]{:S(2)}) async-start(bf16[64,16,128]{2,1,0:T(8,128)(2,1)} %get-tuple-element.15), calls=%async_computation.2 | async-start | bytes 524288 | tf_op jit(solution)/shard_map/all_to_all | solution.py:278
  98.8 3.3 %collective-permute-start.1 = (f32[2,16,128]{2,1,0:T(8,128)S(1)}, f32[2,16,128]{2,1,0:T(8,128)S(1)}, u32[]{:S(2)}, u32[]{:S(2)}) collective-permute-start(f32[2,16,128]{2,1,0:T(8,128)S(1)} %slice.9), channel_id=1, source_target_pairs={{0,32},{32,0},{1,33},{33,1},{2,34},{34,2},{3,35},{35,3},{4,36},{36... | collective-permute-start | bytes 49160 | tf_op jit(solution)/shard_map/ppermute | solution.py:344
  102.1 1.8 %collective-permute-done.1.along_ref = f32[2,16,128]{2,1,0:T(8,128)S(1)} collective-permute-done((f32[2,16,128]{2,1,0:T(8,128)S(1)}, f32[2,16,128]{2,1,0:T(8,128)S(1)}, u32[]{:S(2)}, u32[]{:S(2)}) %collective-permute-start.1) | collective-permute-done | bytes 16416 | tf_op jit(solution)/shard_map/ppermute | solution.py:344
  104.0 2.8 %collective-permute-start.2 = (f32[2,16,128]{2,1,0:T(8,128)S(1)}, f32[2,16,128]{2,1,0:T(8,128)S(1)}, u32[]{:S(2)}, u32[]{:S(2)}) collective-permute-start(f32[2,16,128]{2,1,0:T(8,128)S(1)} %pad_maximum_fusion), channel_id=1, source_target_pairs={{0,16},{16,0},{1,17},{17,1},{2,18},{18,2},{3,19},{19,3},{4,20},{20... | collective-permute-start | bytes 49160 | tf_op jit(solution)/shard_map/ppermute | solution.py:344
  106.8 0.8 collective-permute-done.2.across_ref
  107.7 0.7 shard_map.71
  108.3 0.6 all-to-all-done.2.in_ref
  109.0 0.9 shard_map.72
  (7 shorter events, 0.0 us)
Async XLA Ops:
  3.4 11.0 %copy-start.2 = (bf16[48,128]{1,0:T(8,128)(2,1)S(1)}, bf16[48,128]{1,0:T(8,128)(2,1)}, u32[]{:S(2)}) copy-start(bf16[48,128]{1,0:T(8,128)(2,1)} %get-tuple-element.11) | copy-start | bytes 36868
  3.4 14.3 %copy-start = (bf16[48,128]{1,0:T(8,128)(2,1)S(1)}, bf16[48,128]{1,0:T(8,128)(2,1)}, u32[]{:S(2)}) copy-start(bf16[48,128]{1,0:T(8,128)(2,1)} %get-tuple-element.10) | copy-start | bytes 36868
  3.5 49.0 %all-to-all-start = ((bf16[64,48,128]{2,1,0:T(8,128)(2,1)}), bf16[64,48,128]{2,1,0:T(8,128)(2,1)S(1)}, u32[]{:S(2)}, u32[]{:S(2)}) async-start(bf16[64,48,128]{2,1,0:T(8,128)(2,1)} %get-tuple-element.9), calls=%async_computation | async-start | bytes 1572864 | tf_op jit(solution)/shard_map/all_to_all | solution.py:278
  14.4 3.3 %collective-permute-start = (bf16[48,128]{1,0:T(8,128)(2,1)S(1)}, bf16[48,128]{1,0:T(8,128)(2,1)S(1)}, u32[]{:S(2)}, u32[]{:S(2)}) collective-permute-start(bf16[48,128]{1,0:T(8,128)(2,1)S(1)} %copy-done.2), channel_id=1, source_target_pairs={{0,16},{16,0},{1,17},{17,1},{2,18},{18,2},{3,19},{19,3},{4,20},{20... | collective-permute-start | bytes 36872 | tf_op jit(solution)/shard_map/ppermute | solution.py:306
  57.8 25.6 %all-to-all-start.1 = ((f32[8,72,128]{2,1,0:T(8,128)}), f32[8,72,128]{2,1,0:T(8,128)S(1)}, u32[]{:S(2)}, u32[]{:S(2)}) async-start(f32[8,72,128]{2,1,0:T(8,128)} %get-tuple-element.12), calls=%async_computation.1 | async-start | bytes 589824 | tf_op jit(solution)/shard_map/all_to_all | solution.py:278
  64.3 0.7 copy-start.1
  87.0 22.0 %all-to-all-start.2 = ((bf16[64,16,128]{2,1,0:T(8,128)(2,1)}), bf16[64,16,128]{2,1,0:T(8,128)(2,1)S(1)}, u32[]{:S(2)}, u32[]{:S(2)}) async-start(bf16[64,16,128]{2,1,0:T(8,128)(2,1)} %get-tuple-element.15), calls=%async_computation.2 | async-start | bytes 524288 | tf_op jit(solution)/shard_map/all_to_all | solution.py:278
  98.8 5.1 %collective-permute-start.1 = (f32[2,16,128]{2,1,0:T(8,128)S(1)}, f32[2,16,128]{2,1,0:T(8,128)S(1)}, u32[]{:S(2)}, u32[]{:S(2)}) collective-permute-start(f32[2,16,128]{2,1,0:T(8,128)S(1)} %slice.9), channel_id=1, source_target_pairs={{0,32},{32,0},{1,33},{33,1},{2,34},{34,2},{3,35},{35,3},{4,36},{36... | collective-permute-start | bytes 49160 | tf_op jit(solution)/shard_map/ppermute | solution.py:344
  104.0 3.7 %collective-permute-start.2 = (f32[2,16,128]{2,1,0:T(8,128)S(1)}, f32[2,16,128]{2,1,0:T(8,128)S(1)}, u32[]{:S(2)}, u32[]{:S(2)}) collective-permute-start(f32[2,16,128]{2,1,0:T(8,128)S(1)} %pad_maximum_fusion), channel_id=1, source_target_pairs={{0,16},{16,0},{1,17},{17,1},{2,18},{18,2},{3,19},{19,3},{4,20},{20... | collective-permute-start | bytes 49160 | tf_op jit(solution)/shard_map/ppermute | solution.py:344

commit v4 on v3

--- a/solution.py
+++ b/solution.py
@@ -105,7 +105,32 @@
     return lax.broadcasted_iota(jnp.int32, shape, rank - 1) < HALF
 
 
-def totals_kernel(chunk, near_ref, keys_ref, rows_ref, out_ref, span_ref, score_ref):
+UNIT = SH + 2
+
+
+def squeeze(means):
+    teach, stud = means[:, :, :UNIT], means[:, :, HALF : HALF + UNIT]
+    rows = means.shape[1]
+    deep = 3 * rows // 4
+    rest = rows - (deep - (rows - deep))
+    none = jnp.zeros_like(stud[:, : deep - rest])
+    second = jnp.concatenate([teach[:, deep:], stud[:, : rows - rest]], axis=1)
+    third = jnp.concatenate([stud[:, rows - rest :], none], axis=1)
+    gap = jnp.zeros(third.shape[:2] + (LANES - 3 * UNIT,), F32)
+    return jnp.concatenate([teach[:, :deep], second, third, gap], axis=2)
+
+
+def spread(packed):
+    deep = packed.shape[1]
+    rows = deep * 4 // 3
+    rest = rows - (deep - (rows - deep))
+    first, second, third = (packed[:, :, k * UNIT : (k + 1) * UNIT] for k in range(3))
+    teach = jnp.concatenate([first, second[:, : rows - deep]], axis=1)
+    stud = jnp.concatenate([second[:, rows - deep :], third[:, :rest]], axis=1)
+    return teach, stud
+
+
+def totals_kernel(chunk, wide, near_ref, keys_ref, rows_ref, out_ref, span_ref, score_ref):
     teach_q, left_q, right_q = queries_of(near_ref, rows_ref)
     span_ref[0], span_ref[1], span_ref[2] = teach_q, left_q, right_q
     queries = teach_q.shape[0]
@@ -113,7 +138,7 @@
     scales = (LOG2E / math.sqrt(TH), LOG2E / math.sqrt(SH))
 
     def measure(index, tops):
-        first, second, pack = key_chunk(keys_ref, index * chunk, chunk)
+        first, second, pack = key_chunk(keys_ref, index * wide, wide)
         here = pl.ds(index * first.shape[0], first.shape[0])
         found = []
         for kind, span, key in ((0, 0, first), (0, 0, second), (1, 1, pack), (1, 2, pack)):
@@ -125,7 +150,7 @@
         )
 
     start = jnp.full((8, queries), -1e30, F32)
-    tops = lax.fori_loop(0, steps, measure, (start, start), unroll=True)
+    tops = lax.fori_loop(0, keys_ref.shape[0] // wide, measure, (start, start), unroll=True)
     tops = [jnp.max(top, axis=0, keepdims=True) * scale for top, scale in zip(tops, scales)]
 
     def gather(index, state):
@@ -169,7 +194,8 @@
         mean = state[2][kind * HALF : kind * HALF + SH] * (1.0 / total)
         columns += [mean, jnp.broadcast_to(log, (HALF - SH, queries))]
     groups, own = out_ref.shape[0], out_ref.shape[1] - 8
-    out_ref[:, :own, :] = jnp.concatenate(columns, axis=0).T.reshape(groups, own, LANES)
+    means = jnp.concatenate(columns, axis=0).T.reshape(groups, queries // groups, LANES)
+    out_ref[:, :own, :] = squeeze(means)
     out_ref[:, own:, :] = jnp.broadcast_to(
         jnp.concatenate(lines, axis=0)[None], (groups, 8, LANES)
     )
@@ -189,11 +215,13 @@
     weights = weights_ref[...]
     own = key_ref.shape[1]
 
-    means = logs_ref[:, :deep, :]
-    each = jnp.where(low_lanes(3), means[:, :, SH : SH + 1], means[:, :, HALF + SH : HALF + SH + 1])
-    share = jnp.exp2(each - jnp.max(each, axis=0, keepdims=True))
-    mean = jnp.sum(share * means, axis=0) / jnp.sum(share, axis=0)
-    mean = (turn(mean) - mean) * own_ref[...] * (1.0 / math.sqrt(SH))
+    found = []
+    for part in spread(logs_ref[:, :deep, :]):
+        each = part[:, :, SH : SH + 1]
+        share = jnp.exp2(each - jnp.max(each, axis=0, keepdims=True))
+        found.append(jnp.sum(share * part, axis=0) / jnp.sum(share, axis=0))
+    mean = (found[1] - found[0]) * own_ref[:, :UNIT] * (1.0 / math.sqrt(SH))
+    mean = jnp.concatenate([mean, jnp.zeros((mean.shape[0], LANES - UNIT), F32)], axis=1)
     mean_ref[...] = mean.reshape(mean_ref.shape)
     spot = near_ref[0] * CORES + core_ref[0]
     for step_to in range(NEAR * CORES):
@@ -322,8 +350,8 @@
 
     deep = queries // groups
     logs, spans = call(
-        functools.partial(totals_kernel, 8),
-        (shape((groups, deep + 8, LANES), F32), shape((3, queries, LANES), BF16)),
+        functools.partial(totals_kernel, 8, 32),
+        (shape((groups, 3 * deep // 4 + 8, LANES), F32), shape((3, queries, LANES), BF16)),
         scratch=[pltpu.VMEM((4, heads * half, queries), F32)],
         smem=1,
         flops=2**31,

time: 110 us -> 108 us (0.982)
  starting transfers between devices: 37.9 us -> 36.4 us
  waiting for transfers between devices: 22.5 us -> 21 us
    all_to_all x3, starting transfers between devices: 29.3 us -> 27.8 us  [trade(): return lax.all_to_all(array, axes, split_axis=0, concat_axis=0, tiled=True)]
    all_to_all x3, waiting for transfers between devices: 19 us -> 17.5 us  [trade(): return lax.all_to_all(array, axes, split_axis=0, concat_axis=0, tiled=True)]
where the time goes in v4:
time: 108 us; the launch traced here: 107 us
  starting transfers between devices  36.4 us (34%)
  blocking collectives  34.7 us (32%)
  waiting for transfers between devices  21 us (19%)
  Pallas kernels  13.3 us (12%)
    all_gather x1, blocking collectives, on_device(): lax.all_gather(shard, ('group', 'near', 'core'), axis=0, tiled=True, axis...  34.7 us
    all_to_all x3, starting transfers between devices, trade(): return lax.all_to_all(array, axes, split_axis=0, concat_axis=0, tiled=True)  27.8 us
    all_to_all x3, waiting for transfers between devices, trade(): return lax.all_to_all(array, axes, split_axis=0, concat_axis=0, tiled=True)  17.5 us
    pallas_call x5, Pallas kernels, run(): pl.pallas_call(body, out_shape=shapes, in_specs=specs((smem, raw, len(arg...  13.3 us
    ppermute x2, starting transfers between devices, on_device(): flip = lambda array, axis: lax.ppermute(array, axis, [(0, 1), (1, 0)])  6.13 us
    ppermute x2, waiting for transfers between devices, on_device(): flip = lambda array, axis: lax.ppermute(array, axis, [(0, 1), (1, 0)])  2.65 us
    ppermute x1, starting transfers between devices, on_device(): other = lax.ppermute(given, 'core', [(0, 1), (1, 0)])  2.48 us
  transfers between devices with their start and end apart: 6, of which 5 were waited for; matrix products, arithmetic and copies ran while one was open for 0% of the time, Pallas kernels for 1%

profile of v4, /device:TPU:1, one launch (start us, length us, event | category | flops | bytes accessed | tf_op | source)
XLA Modules:
  0.0 107.0 jit_solution(13553943630005250016)
XLA Ops:
  0.6 2.8 %shard_map.68 = (bf16[64,48,128]{2,1,0:T(8,128)(2,1)}, bf16[48,128]{1,0:T(8,128)(2,1)}, bf16[48,128]{1,0:T(8,128)(2,1)}) custom-call(s32[1]{0:T(128)S(6)} %xor.3.side_ref, bf16[16,512]{1,0:T(8,128)(2,1)} %tq_hbm.1, bf16[32,8192]{1,0:T(8,128)(2,1)} %tk_hbm.1, bf16[16,160]{1,0:T(8,128)(2,1)} %sq_hbm.1, bf16[32,2560]{1,0:T(8,128)(2,1)} %sk_hbm.1), custom_call_target="tpu_custom_call" | custom-call | bytes 709636 | tf_op jit(solution)/shard_map/pallas_call | solution.py:283
  3.4 0.0 copy-start.2
  3.4 0.0 copy-start
  3.5 11.0 %all-to-all-start = ((bf16[64,48,128]{2,1,0:T(8,128)(2,1)}), bf16[64,48,128]{2,1,0:T(8,128)(2,1)S(1)}, u32[]{:S(2)}, u32[]{:S(2)}) async-start(bf16[64,48,128]{2,1,0:T(8,128)(2,1)} %get-tuple-element.9), calls=%async_computation | async-start | bytes 1572864 | tf_op jit(solution)/shard_map/all_to_all | solution.py:306
  14.4 0.0 copy-done.2
  14.4 2.5 %collective-permute-start = (bf16[48,128]{1,0:T(8,128)(2,1)S(1)}, bf16[48,128]{1,0:T(8,128)(2,1)S(1)}, u32[]{:S(2)}, u32[]{:S(2)}) collective-permute-start(bf16[48,128]{1,0:T(8,128)(2,1)S(1)} %copy-done.2), channel_id=1, source_target_pairs={{0,16},{16,0},{1,17},{17,1},{2,18},{18,2},{3,19},{19,3},{4,20},{20... | collective-permute-start | bytes 36872 | tf_op jit(solution)/shard_map/ppermute | solution.py:334
  16.9 0.8 collective-permute-done
  17.7 0.0 copy-done
  17.8 34.7 %all_gather.3.rows_ref = bf16[16,96,128]{2,1,0:T(8,128)(2,1)S(1)} all-gather(bf16[1,96,128]{2,1,0:T(8,128)(2,1)S(1)} %bitcast.7), channel_id=1, replica_groups={{0,48,64,112,128,176,192,240,256,304,320,368,384,432,448,496},{16,32,80..., dimensions={0}, use_global_device_ids=true | all-gather | bytes 417792 | tf_op jit(solution)/shard_map/all_gather | solution.py:341
  52.4 0.0 all-to-all-done.keys_ref
  52.5 5.4 %shard_map.69 = (f32[8,56,128]{2,1,0:T(8,128)}, bf16[3,512,128]{2,1,0:T(8,128)(2,1)S(1)}) custom-call(s32[1]{0:T(128)} %bitcast.near_ref, bf16[64,48,128]{2,1,0:T(8,128)(2,1)S(1)} %all-to-all-done.keys_ref, bf16[16,96,128]{2,1,0:T(8,128)(2,1)S(1)} %all_gather.3.rows_ref), custom_call_target="tpu_custom_call" | custom-call | flops 2147483648 | bytes 1179652 | tf_op jit(solution)/shard_map/pallas_call | solution.py:283
  57.8 6.5 %all-to-all-start.1 = ((f32[8,56,128]{2,1,0:T(8,128)}), f32[8,56,128]{2,1,0:T(8,128)S(1)}, u32[]{:S(2)}, u32[]{:S(2)}) async-start(f32[8,56,128]{2,1,0:T(8,128)} %get-tuple-element.12), calls=%async_computation.1 | async-start | bytes 458752 | tf_op jit(solution)/shard_map/all_to_all | solution.py:306
  64.3 0.0 copy-start.1
  64.3 0.7 copy-done.1
  65.0 0.1 dynamic_slice.3
  65.1 16.9 %all-to-all-done.1.logs_ref = f32[8,56,128]{2,1,0:T(8,128)S(1)} async-done(((f32[8,56,128]{2,1,0:T(8,128)}), f32[8,56,128]{2,1,0:T(8,128)S(1)}, u32[]{:S(2)}, u32[]{:S(2)}) %all-to-all-start.1) | async-done | bytes 229408 | tf_op jit(solution)/shard_map/all_to_all | solution.py:306
  82.0 0.1 broadcast_in_dim.2.own_ref
  82.0 3.6 %shard_map.70 = (bf16[64,16,128]{2,1,0:T(8,128)(2,1)}, f32[4,16,128]{2,1,0:T(8,128)S(1)}) custom-call(s32[1]{0:T(128)} %bitcast.near_ref, s32[1]{0:T(128)} %bitcast.1.core_ref, f32[8,56,128]{2,1,0:T(8,128)S(1)} %all-to-all-done.1.logs_ref, f32[1,512]{1,0:T(1,128)S(1)} %bitcast.6, f32[64,128]{1,0:T(8,128)S(1)} %broadcast_in_dim.2.own_ref, ...), custom_call_target="tpu_custom_call" | custom-call | flops 1073741824 | bytes 1443848 | tf_op jit(solution)/shard_map/pallas_call | solution.py:283
  85.6 10.3 %all-to-all-start.2 = ((bf16[64,16,128]{2,1,0:T(8,128)(2,1)}), bf16[64,16,128]{2,1,0:T(8,128)(2,1)S(1)}, u32[]{:S(2)}, u32[]{:S(2)}) async-start(bf16[64,16,128]{2,1,0:T(8,128)(2,1)} %get-tuple-element.15), calls=%async_computation.2 | async-start | bytes 524288 | tf_op jit(solution)/shard_map/all_to_all | solution.py:306
  96.0 3.3 %collective-permute-start.1 = (f32[2,16,128]{2,1,0:T(8,128)S(1)}, f32[2,16,128]{2,1,0:T(8,128)S(1)}, u32[]{:S(2)}, u32[]{:S(2)}) collective-permute-start(f32[2,16,128]{2,1,0:T(8,128)S(1)} %slice.9), channel_id=1, source_target_pairs={{0,32},{32,0},{1,33},{33,1},{2,34},{34,2},{3,35},{35,3},{4,36},{36... | collective-permute-start | bytes 49160 | tf_op jit(solution)/shard_map/ppermute | solution.py:372
  99.3 1.8 %collective-permute-done.1.along_ref = f32[2,16,128]{2,1,0:T(8,128)S(1)} collective-permute-done((f32[2,16,128]{2,1,0:T(8,128)S(1)}, f32[2,16,128]{2,1,0:T(8,128)S(1)}, u32[]{:S(2)}, u32[]{:S(2)}) %collective-permute-start.1) | collective-permute-done | bytes 16416 | tf_op jit(solution)/shard_map/ppermute | solution.py:372
  101.1 2.8 %collective-permute-start.2 = (f32[2,16,128]{2,1,0:T(8,128)S(1)}, f32[2,16,128]{2,1,0:T(8,128)S(1)}, u32[]{:S(2)}, u32[]{:S(2)}) collective-permute-start(f32[2,16,128]{2,1,0:T(8,128)S(1)} %pad_maximum_fusion), channel_id=1, source_target_pairs={{0,16},{16,0},{1,17},{17,1},{2,18},{18,2},{3,19},{19,3},{4,20},{20... | collective-permute-start | bytes 49160 | tf_op jit(solution)/shard_map/ppermute | solution.py:372
  104.0 0.8 collective-permute-done.2.across_ref
  104.8 0.7 shard_map.71
  105.5 0.6 all-to-all-done.2.in_ref
  106.1 0.9 shard_map.72
  (7 shorter events, 0.0 us)
Async XLA Ops:
  3.4 11.0 %copy-start.2 = (bf16[48,128]{1,0:T(8,128)(2,1)S(1)}, bf16[48,128]{1,0:T(8,128)(2,1)}, u32[]{:S(2)}) copy-start(bf16[48,128]{1,0:T(8,128)(2,1)} %get-tuple-element.11) | copy-start | bytes 36868
  3.4 14.3 %copy-start = (bf16[48,128]{1,0:T(8,128)(2,1)S(1)}, bf16[48,128]{1,0:T(8,128)(2,1)}, u32[]{:S(2)}) copy-start(bf16[48,128]{1,0:T(8,128)(2,1)} %get-tuple-element.10) | copy-start | bytes 36868
  3.5 49.0 %all-to-all-start = ((bf16[64,48,128]{2,1,0:T(8,128)(2,1)}), bf16[64,48,128]{2,1,0:T(8,128)(2,1)S(1)}, u32[]{:S(2)}, u32[]{:S(2)}) async-start(bf16[64,48,128]{2,1,0:T(8,128)(2,1)} %get-tuple-element.9), calls=%async_computation | async-start | bytes 1572864 | tf_op jit(solution)/shard_map/all_to_all | solution.py:306
  14.4 3.3 %collective-permute-start = (bf16[48,128]{1,0:T(8,128)(2,1)S(1)}, bf16[48,128]{1,0:T(8,128)(2,1)S(1)}, u32[]{:S(2)}, u32[]{:S(2)}) collective-permute-start(bf16[48,128]{1,0:T(8,128)(2,1)S(1)} %copy-done.2), channel_id=1, source_target_pairs={{0,16},{16,0},{1,17},{17,1},{2,18},{18,2},{3,19},{19,3},{4,20},{20... | collective-permute-start | bytes 36872 | tf_op jit(solution)/shard_map/ppermute | solution.py:334
  57.8 24.1 %all-to-all-start.1 = ((f32[8,56,128]{2,1,0:T(8,128)}), f32[8,56,128]{2,1,0:T(8,128)S(1)}, u32[]{:S(2)}, u32[]{:S(2)}) async-start(f32[8,56,128]{2,1,0:T(8,128)} %get-tuple-element.12), calls=%async_computation.1 | async-start | bytes 458752 | tf_op jit(solution)/shard_map/all_to_all | solution.py:306
  64.3 0.7 copy-start.1
  85.6 20.5 %all-to-all-start.2 = ((bf16[64,16,128]{2,1,0:T(8,128)(2,1)}), bf16[64,16,128]{2,1,0:T(8,128)(2,1)S(1)}, u32[]{:S(2)}, u32[]{:S(2)}) async-start(bf16[64,16,128]{2,1,0:T(8,128)(2,1)} %get-tuple-element.15), calls=%async_computation.2 | async-start | bytes 524288 | tf_op jit(solution)/shard_map/all_to_all | solution.py:306
  96.0 5.1 %collective-permute-start.1 = (f32[2,16,128]{2,1,0:T(8,128)S(1)}, f32[2,16,128]{2,1,0:T(8,128)S(1)}, u32[]{:S(2)}, u32[]{:S(2)}) collective-permute-start(f32[2,16,128]{2,1,0:T(8,128)S(1)} %slice.9), channel_id=1, source_target_pairs={{0,32},{32,0},{1,33},{33,1},{2,34},{34,2},{3,35},{35,3},{4,36},{36... | collective-permute-start | bytes 49160 | tf_op jit(solution)/shard_map/ppermute | solution.py:372
  101.1 3.7 %collective-permute-start.2 = (f32[2,16,128]{2,1,0:T(8,128)S(1)}, f32[2,16,128]{2,1,0:T(8,128)S(1)}, u32[]{:S(2)}, u32[]{:S(2)}) collective-permute-start(f32[2,16,128]{2,1,0:T(8,128)S(1)} %pad_maximum_fusion), channel_id=1, source_target_pairs={{0,16},{16,0},{1,17},{17,1},{2,18},{18,2},{3,19},{19,3},{4,20},{20... | collective-permute-start | bytes 49160 | tf_op jit(solution)/shard_map/ppermute | solution.py:372

commit v5 on v4

--- a/solution.py
+++ b/solution.py
@@ -24,7 +24,7 @@
     return jnp.concatenate([low, gap, high, gap], axis=1)
 
 
-def pack(side_ref, tq_hbm, tk_hbm, sq_hbm, sk_hbm, keys_hbm, kept_ref, given_ref,
+def pack(side_ref, turn_ref, tq_hbm, tk_hbm, sq_hbm, sk_hbm, keys_hbm, kept_ref, given_ref,
          tq_ref, tk_ref, sq_ref, sk_ref, keys_ref, sems):
     heads, tokens, half = keys_hbm.shape[0], tk_hbm.shape[0], tk_hbm.shape[0] // 2
     fetches = [
@@ -54,13 +54,13 @@
     fetches[2].wait()
     for head in range(heads):
         part = sk_ref[:, head * SH : (head + 1) * SH]
-        keys_ref[head, tokens:, :] = side_by_side(part[:half], part[half:])
+        keys_ref[head ^ turn_ref[0], tokens:, :] = side_by_side(part[:half], part[half:])
     fetches[3].wait()
     group = heads // 4
     sends = []
     for start in range(0, heads, group):
         for head in range(start, start + group):
-            keys_ref[head, :tokens, :] = tk_ref[:, head * TH : (head + 1) * TH]
+            keys_ref[head ^ turn_ref[0], :tokens, :] = tk_ref[:, head * TH : (head + 1) * TH]
         here = pl.ds(start, group)
         sends.append(
             pltpu.make_async_copy(keys_ref.at[here], keys_hbm.at[here], sems.at[4 + start // group])
@@ -245,13 +245,13 @@
     lax.fori_loop(0, keys_ref.shape[0] // chunk, step, 0, unroll=True)
 
 
-def unpack_keys(in_ref, out_ref):
+def unpack_keys(turn_ref, in_ref, out_ref):
     half = in_ref.shape[1]
     group = 16
     for start in range(0, in_ref.shape[0], group):
         for side in range(2):
             parts = [
-                in_ref[head, :, side * HALF : side * HALF + SH].astype(F32)
+                in_ref[head ^ turn_ref[0], :, side * HALF : side * HALF + SH].astype(F32)
                 for head in range(start, start + group)
             ]
             out_ref[side * half : (side + 1) * half, start * SH : (start + group) * SH] = (
@@ -259,8 +259,8 @@
             )
 
 
-def unpack_rows(near_ref, core_ref, mine_ref, along_ref, across_ref, out_ref, part_ref):
-    spot = near_ref[0] * CORES + core_ref[0]
+def unpack_rows(near_ref, core_ref, turn_ref, mine_ref, along_ref, across_ref, out_ref, part_ref):
+    spot = (near_ref[0] * CORES + core_ref[0]) ^ turn_ref[0]
     part_ref[spot] = mine_ref[0]
     part_ref[spot ^ 2] = along_ref[0]
     part_ref[spot ^ 1] = across_ref[0]
@@ -293,6 +293,10 @@
     return run
 
 
+def alternate(places):
+    return [[z * CORES + (core ^ flip) for z, core in places] for flip in range(CORES)]
+
+
 def on_device(teacher_span, teacher_context, student_span, student_context, query_weights):
     groups, tps = lax.axis_size("group"), lax.axis_size("tp")
     heads = tps * NEAR * CORES
@@ -307,6 +311,7 @@
 
     core = lax.axis_index("core").astype(jnp.int32)
     side = core.reshape(1)
+    odd = (lax.axis_index("group") % 2).astype(jnp.int32).reshape(1)
     spot = lax.axis_index("near").astype(jnp.int32).reshape(1)
     piece = shape(((NEAR + 1) * rows_own, LANES), BF16)
     keys, kept, given = call(
@@ -320,12 +325,13 @@
             pltpu.VMEM((heads, 3 * half, LANES), BF16),
             pltpu.SemaphoreType.DMA((8,)),
         ],
-        smem=1,
+        smem=2,
         raw=4,
         raw_out=1,
         room=62,
     )(
-        spot ^ side,
+        spot ^ side ^ odd,
+        odd,
         teacher_span,
         teacher_context,
         student_span,
@@ -343,9 +349,9 @@
         ("group", "near", "core"),
         axis=0,
         tiled=True,
-        axis_index_groups=[
-            [z * CORES + (z + side) % CORES for z in range(groups * NEAR)] for side in range(CORES)
-        ],
+        axis_index_groups=alternate(
+            [(z, z % NEAR ^ z // NEAR % 2) for z in range(groups * NEAR)]
+        ),
     )
 
     deep = queries // groups
@@ -356,13 +362,24 @@
         smem=1,
         flops=2**31,
     )(spot, keys, rows)
-    logs = trade(logs, "group")
+    logs = lax.all_to_all(
+        logs,
+        ("group", "near", "core"),
+        split_axis=0,
+        concat_axis=0,
+        tiled=True,
+        axis_index_groups=[
+            members
+            for spot_in in range(NEAR)
+            for members in alternate([(z * NEAR + spot_in, z % 2) for z in range(groups)])
+        ],
+    )
     tokens_all = tokens_own * heads * groups
     weights = math.sqrt(tokens_all) * query_weights
     own = lax.dynamic_slice(weights, (lax.axis_index("group") * deep,), (deep,))
     own = jnp.broadcast_to(own[:, None], (deep, LANES))
     parts, mine = call(
-        functools.partial(grads_kernel, 8),
+        functools.partial(grads_kernel, 32),
         (shape((heads, half, LANES), BF16), shape((near, rows_own, LANES), F32)),
         scratch=[pltpu.VMEM((near, rows_own, LANES), F32)],
         smem=2,
@@ -376,9 +393,9 @@
         unpack_rows,
         shape((rows_own, near * SH), F32),
         scratch=[pltpu.VMEM((near, rows_own, LANES), F32)],
-        smem=2,
-    )(spot, side, mine, along, across)
-    grad_context = call(unpack_keys, shape((tokens_own, heads * SH), F32))(parts)
+        smem=3,
+    )(spot, side, odd, mine, along, across)
+    grad_context = call(unpack_keys, shape((tokens_own, heads * SH), F32), smem=1)(odd, parts)
     return (grad_span, grad_context)
 
 

time: 108 us -> 107 us (level)
  starting transfers between devices: 36.4 us -> 39.6 us
  waiting for transfers between devices: 21 us -> 19.3 us
  blocking collectives: 34.7 us -> 33.3 us
    all_to_all x3 -> x2, waiting for transfers between devices: 17.5 us -> 0.65 us  [trade(): return lax.all_to_all(array, axes, split_axis=0, concat_axis=0, tiled=True)]
    all_to_all x0 -> x1, waiting for transfers between devices: none -> 15.2 us  [on_device(): lax.all_to_all(logs, ('group', 'near', 'core'), split_axis=0, concat_axis...]
    all_to_all x0 -> x1, starting transfers between devices: none -> 6.33 us  [on_device(): lax.all_to_all(logs, ('group', 'near', 'core'), split_axis=0, concat_axis...]
    all_to_all x3 -> x2, starting transfers between devices: 27.8 us -> 24.6 us  [trade(): return lax.all_to_all(array, axes, split_axis=0, concat_axis=0, tiled=True)]
    all_gather x1, blocking collectives: 34.7 us -> 33.3 us  [on_device(): lax.all_gather(shard, ('group', 'near', 'core'), axis=0, tiled=True, axis...]
where the time goes in v5:
time: 107 us
  starting transfers between devices  39.6 us (37%)
  blocking collectives  33.3 us (31%)
  waiting for transfers between devices  19.3 us (18%)
  Pallas kernels  12.8 us (12%)
    all_gather x1, blocking collectives, on_device(): lax.all_gather(shard, ('group', 'near', 'core'), axis=0, tiled=True, axis...  33.3 us
    all_to_all x2, starting transfers between devices, trade(): return lax.all_to_all(array, axes, split_axis=0, concat_axis=0, tiled=True)  24.6 us
    all_to_all x1, waiting for transfers between devices, on_device(): lax.all_to_all(logs, ('group', 'near', 'core'), split_axis=0, concat_axis...  15.2 us
    pallas_call x5, Pallas kernels, run(): pl.pallas_call(body, out_shape=shapes, in_specs=specs((smem, raw, len(arg...  12.8 us
    all_to_all x1, starting transfers between devices, on_device(): lax.all_to_all(logs, ('group', 'near', 'core'), split_axis=0, concat_axis...  6.33 us
    ppermute x2, starting transfers between devices, on_device(): flip = lambda array, axis: lax.ppermute(array, axis, [(0, 1), (1, 0)])  6.13 us
    ppermute x2, waiting for transfers between devices, on_device(): flip = lambda array, axis: lax.ppermute(array, axis, [(0, 1), (1, 0)])  2.65 us
    ppermute x1, starting transfers between devices, on_device(): other = lax.ppermute(given, 'core', [(0, 1), (1, 0)])  2.48 us
  transfers between devices with their start and end apart: 6, of which 5 were waited for; matrix products, arithmetic and copies ran while one was open for 0% of the time, Pallas kernels for 1%

profile of v5, /device:TPU:1, one launch (start us, length us, event | category | flops | bytes accessed | tf_op | source)
XLA Modules:
  0.0 106.6 jit_solution(9258894295164420597)
XLA Ops:
  0.6 2.8 %shard_map.68 = (bf16[64,48,128]{2,1,0:T(8,128)(2,1)}, bf16[48,128]{1,0:T(8,128)(2,1)}, bf16[48,128]{1,0:T(8,128)(2,1)}) custom-call(s32[1]{0:T(128)S(6)} %xor.7.side_ref, s32[1]{0:T(128)} %bitcast.2.turn_ref, bf16[16,512]{1,0:T(8,128)(2,1)} %tq_hbm.1, bf16[32,8192]{1,0:T(8,128)(2,1)} %tk_hbm.1, bf16[16,160]{1,0:T(8,128)(2,1)} %sq_hbm.1, bf16[32,2560]{1,0:T(8,128)(2,1)} %sk_hbm.1), custom_call_target="tpu_custom_call" | custom-call | bytes 709640 | tf_op jit(solution)/shard_map/pallas_call | solution.py:283
  3.4 0.0 copy-start.2
  3.5 0.0 copy-start
  3.5 11.0 %all-to-all-start = ((bf16[64,48,128]{2,1,0:T(8,128)(2,1)}), bf16[64,48,128]{2,1,0:T(8,128)(2,1)S(1)}, u32[]{:S(2)}, u32[]{:S(2)}) async-start(bf16[64,48,128]{2,1,0:T(8,128)(2,1)} %get-tuple-element.9), calls=%async_computation | async-start | bytes 1572864 | tf_op jit(solution)/shard_map/all_to_all | solution.py:310
  14.4 0.0 copy-done.2
  14.5 2.5 %collective-permute-start = (bf16[48,128]{1,0:T(8,128)(2,1)S(1)}, bf16[48,128]{1,0:T(8,128)(2,1)S(1)}, u32[]{:S(2)}, u32[]{:S(2)}) collective-permute-start(bf16[48,128]{1,0:T(8,128)(2,1)S(1)} %copy-done.2), channel_id=1, source_target_pairs={{0,16},{16,0},{1,17},{17,1},{2,18},{18,2},{3,19},{19,3},{4,20},{20... | collective-permute-start | bytes 36872 | tf_op jit(solution)/shard_map/ppermute | solution.py:340
  16.9 0.8 collective-permute-done
  17.7 0.0 copy-done
  17.8 33.3 %all_gather.3.rows_ref = bf16[16,96,128]{2,1,0:T(8,128)(2,1)S(1)} all-gather(bf16[1,96,128]{2,1,0:T(8,128)(2,1)S(1)} %bitcast.8), channel_id=1, replica_groups={{0,48,80,96,128,176,208,224,256,304,336,352,384,432,464,480},{16,32,64,..., dimensions={0}, use_global_device_ids=true | all-gather | bytes 417792 | tf_op jit(solution)/shard_map/all_gather | solution.py:347
  51.1 0.0 all-to-all-done.keys_ref
  51.1 5.4 %shard_map.69 = (f32[8,56,128]{2,1,0:T(8,128)}, bf16[3,512,128]{2,1,0:T(8,128)(2,1)S(1)}) custom-call(s32[1]{0:T(128)} %bitcast.near_ref, bf16[64,48,128]{2,1,0:T(8,128)(2,1)S(1)} %all-to-all-done.keys_ref, bf16[16,96,128]{2,1,0:T(8,128)(2,1)S(1)} %all_gather.3.rows_ref), custom_call_target="tpu_custom_call" | custom-call | flops 2147483648 | bytes 1179652 | tf_op jit(solution)/shard_map/pallas_call | solution.py:283
  56.5 6.3 %all-to-all-start.1 = ((f32[8,56,128]{2,1,0:T(8,128)}), f32[8,56,128]{2,1,0:T(8,128)S(1)}, u32[]{:S(2)}, u32[]{:S(2)}) async-start(f32[8,56,128]{2,1,0:T(8,128)} %get-tuple-element.12), calls=%async_computation.1 | async-start | bytes 458752 | tf_op jit(solution)/shard_map/all_to_all | solution.py:365
  62.8 0.0 copy-start.1
  62.8 0.7 copy-done.1
  63.5 0.1 dynamic_slice.3
  63.6 15.2 %all-to-all-done.1.logs_ref = f32[8,56,128]{2,1,0:T(8,128)S(1)} async-done(((f32[8,56,128]{2,1,0:T(8,128)}), f32[8,56,128]{2,1,0:T(8,128)S(1)}, u32[]{:S(2)}, u32[]{:S(2)}) %all-to-all-start.1) | async-done | bytes 229408 | tf_op jit(solution)/shard_map/all_to_all | solution.py:365
  78.7 0.1 broadcast_in_dim.2.own_ref
  78.8 3.0 %shard_map.70 = (bf16[64,16,128]{2,1,0:T(8,128)(2,1)}, f32[4,16,128]{2,1,0:T(8,128)S(1)}) custom-call(s32[1]{0:T(128)} %bitcast.near_ref, s32[1]{0:T(128)} %bitcast.1.core_ref, f32[8,56,128]{2,1,0:T(8,128)S(1)} %all-to-all-done.1.logs_ref, f32[1,512]{1,0:T(1,128)S(1)} %bitcast.7, f32[64,128]{1,0:T(8,128)S(1)} %broadcast_in_dim.2.own_ref, ...), custom_call_target="tpu_custom_call" | custom-call | flops 1073741824 | bytes 1443848 | tf_op jit(solution)/shard_map/pallas_call | solution.py:283
  81.8 13.7 %all-to-all-start.2 = ((bf16[64,16,128]{2,1,0:T(8,128)(2,1)}), bf16[64,16,128]{2,1,0:T(8,128)(2,1)S(1)}, u32[]{:S(2)}, u32[]{:S(2)}) async-start(bf16[64,16,128]{2,1,0:T(8,128)(2,1)} %get-tuple-element.15), calls=%async_computation.2 | async-start | bytes 524288 | tf_op jit(solution)/shard_map/all_to_all | solution.py:310
  95.5 3.3 %collective-permute-start.1 = (f32[2,16,128]{2,1,0:T(8,128)S(1)}, f32[2,16,128]{2,1,0:T(8,128)S(1)}, u32[]{:S(2)}, u32[]{:S(2)}) collective-permute-start(f32[2,16,128]{2,1,0:T(8,128)S(1)} %slice.9), channel_id=1, source_target_pairs={{0,32},{32,0},{1,33},{33,1},{2,34},{34,2},{3,35},{35,3},{4,36},{36... | collective-permute-start | bytes 49160 | tf_op jit(solution)/shard_map/ppermute | solution.py:389
  98.8 1.8 %collective-permute-done.1.along_ref = f32[2,16,128]{2,1,0:T(8,128)S(1)} collective-permute-done((f32[2,16,128]{2,1,0:T(8,128)S(1)}, f32[2,16,128]{2,1,0:T(8,128)S(1)}, u32[]{:S(2)}, u32[]{:S(2)}) %collective-permute-start.1) | collective-permute-done | bytes 16416 | tf_op jit(solution)/shard_map/ppermute | solution.py:389
  100.6 2.8 %collective-permute-start.2 = (f32[2,16,128]{2,1,0:T(8,128)S(1)}, f32[2,16,128]{2,1,0:T(8,128)S(1)}, u32[]{:S(2)}, u32[]{:S(2)}) collective-permute-start(f32[2,16,128]{2,1,0:T(8,128)S(1)} %pad_maximum_fusion), channel_id=1, source_target_pairs={{0,16},{16,0},{1,17},{17,1},{2,18},{18,2},{3,19},{19,3},{4,20},{20... | collective-permute-start | bytes 49160 | tf_op jit(solution)/shard_map/ppermute | solution.py:389
  103.5 0.8 collective-permute-done.2.across_ref
  104.3 0.7 shard_map.71
  105.0 0.6 all-to-all-done.2.in_ref
  105.6 0.9 shard_map.72
  (7 shorter events, 0.0 us)
Async XLA Ops:
  3.4 11.0 %copy-start.2 = (bf16[48,128]{1,0:T(8,128)(2,1)S(1)}, bf16[48,128]{1,0:T(8,128)(2,1)}, u32[]{:S(2)}) copy-start(bf16[48,128]{1,0:T(8,128)(2,1)} %get-tuple-element.11) | copy-start | bytes 36868
  3.5 14.3 %copy-start = (bf16[48,128]{1,0:T(8,128)(2,1)S(1)}, bf16[48,128]{1,0:T(8,128)(2,1)}, u32[]{:S(2)}) copy-start(bf16[48,128]{1,0:T(8,128)(2,1)} %get-tuple-element.10) | copy-start | bytes 36868
  3.5 47.6 %all-to-all-start = ((bf16[64,48,128]{2,1,0:T(8,128)(2,1)}), bf16[64,48,128]{2,1,0:T(8,128)(2,1)S(1)}, u32[]{:S(2)}, u32[]{:S(2)}) async-start(bf16[64,48,128]{2,1,0:T(8,128)(2,1)} %get-tuple-element.9), calls=%async_computation | async-start | bytes 1572864 | tf_op jit(solution)/shard_map/all_to_all | solution.py:310
  14.5 3.3 %collective-permute-start = (bf16[48,128]{1,0:T(8,128)(2,1)S(1)}, bf16[48,128]{1,0:T(8,128)(2,1)S(1)}, u32[]{:S(2)}, u32[]{:S(2)}) collective-permute-start(bf16[48,128]{1,0:T(8,128)(2,1)S(1)} %copy-done.2), channel_id=1, source_target_pairs={{0,16},{16,0},{1,17},{17,1},{2,18},{18,2},{3,19},{19,3},{4,20},{20... | collective-permute-start | bytes 36872 | tf_op jit(solution)/shard_map/ppermute | solution.py:340
  56.5 22.3 %all-to-all-start.1 = ((f32[8,56,128]{2,1,0:T(8,128)}), f32[8,56,128]{2,1,0:T(8,128)S(1)}, u32[]{:S(2)}, u32[]{:S(2)}) async-start(f32[8,56,128]{2,1,0:T(8,128)} %get-tuple-element.12), calls=%async_computation.1 | async-start | bytes 458752 | tf_op jit(solution)/shard_map/all_to_all | solution.py:365
  62.8 0.7 copy-start.1
  81.8 23.8 %all-to-all-start.2 = ((bf16[64,16,128]{2,1,0:T(8,128)(2,1)}), bf16[64,16,128]{2,1,0:T(8,128)(2,1)S(1)}, u32[]{:S(2)}, u32[]{:S(2)}) async-start(bf16[64,16,128]{2,1,0:T(8,128)(2,1)} %get-tuple-element.15), calls=%async_computation.2 | async-start | bytes 524288 | tf_op jit(solution)/shard_map/all_to_all | solution.py:310
  95.5 5.1 %collective-permute-start.1 = (f32[2,16,128]{2,1,0:T(8,128)S(1)}, f32[2,16,128]{2,1,0:T(8,128)S(1)}, u32[]{:S(2)}, u32[]{:S(2)}) collective-permute-start(f32[2,16,128]{2,1,0:T(8,128)S(1)} %slice.9), channel_id=1, source_target_pairs={{0,32},{32,0},{1,33},{33,1},{2,34},{34,2},{3,35},{35,3},{4,36},{36... | collective-permute-start | bytes 49160 | tf_op jit(solution)/shard_map/ppermute | solution.py:389
  100.6 3.7 %collective-permute-start.2 = (f32[2,16,128]{2,1,0:T(8,128)S(1)}, f32[2,16,128]{2,1,0:T(8,128)S(1)}, u32[]{:S(2)}, u32[]{:S(2)}) collective-permute-start(f32[2,16,128]{2,1,0:T(8,128)S(1)} %pad_maximum_fusion), channel_id=1, source_target_pairs={{0,16},{16,0},{1,17},{17,1},{2,18},{18,2},{3,19},{19,3},{4,20},{20... | collective-permute-start | bytes 49160 | tf_op jit(solution)/shard_map/ppermute | solution.py:389

commit v6 on v5

--- a/solution.py
+++ b/solution.py
@@ -130,33 +130,29 @@
     return teach, stud
 
 
-def totals_kernel(chunk, wide, near_ref, keys_ref, rows_ref, out_ref, span_ref, score_ref):
+def totals_kernel(chunk, near_ref, keys_ref, rows_ref, out_ref, span_ref):
     teach_q, left_q, right_q = queries_of(near_ref, rows_ref)
     span_ref[0], span_ref[1], span_ref[2] = teach_q, left_q, right_q
     queries = teach_q.shape[0]
-    steps = keys_ref.shape[0] // chunk
     scales = (LOG2E / math.sqrt(TH), LOG2E / math.sqrt(SH))
 
-    def measure(index, tops):
-        first, second, pack = key_chunk(keys_ref, index * wide, wide)
-        here = pl.ds(index * first.shape[0], first.shape[0])
-        found = []
-        for kind, span, key in ((0, 0, first), (0, 0, second), (1, 1, pack), (1, 2, pack)):
-            score = scores_of(span_ref[span], key)
-            score_ref[len(found), here] = score
-            found.append(jnp.max(score.reshape(-1, 8, queries), axis=0))
-        return jnp.maximum(tops[0], jnp.maximum(found[0], found[1])), jnp.maximum(
-            tops[1], jnp.maximum(found[2], found[3])
-        )
-
-    start = jnp.full((8, queries), -1e30, F32)
-    tops = lax.fori_loop(0, keys_ref.shape[0] // wide, measure, (start, start), unroll=True)
-    tops = [jnp.max(top, axis=0, keepdims=True) * scale for top, scale in zip(tops, scales)]
-
-    def gather(index, state):
-        sums, means = list(state[:2]), state[2]
-        _, _, pack = key_chunk(keys_ref, index * chunk, chunk)
-        here = pl.ds(index * pack.shape[0], pack.shape[0])
+    def step(index, state):
+        old, sums, means = state[:2], list(state[2:4]), state[4]
+        first, second, pack = key_chunk(keys_ref, index * chunk, chunk)
+        scores = [
+            scores_of(span_ref[span], key) * scales[span > 0]
+            for span, key in ((0, first), (0, second), (1, pack), (2, pack))
+        ]
+        tops = [
+            jnp.maximum(
+                old[kind],
+                jnp.max(
+                    jnp.maximum(scores[2 * kind], scores[2 * kind + 1]), axis=0, keepdims=True
+                ),
+            )
+            for kind in range(2)
+        ]
+        fades = [jnp.exp2(old[kind] - tops[kind]) for kind in range(2)]
         low = low_lanes(2)
         none = jnp.zeros_like(pack)
         turned = turn(pack.astype(F32)).astype(BF16)
@@ -169,23 +165,27 @@
         left, right = [], []
         for number in range(4):
             kind = number // 2
-            prob = jnp.exp2(score_ref[number, here] * scales[kind] - tops[kind])
+            if number % 2 == 0:
+                sums[kind] = sums[kind] * fades[kind]
+            prob = jnp.exp2(scores[number] - tops[kind])
             sums[kind] = sums[kind] + jnp.sum(prob.reshape(-1, 8, queries), axis=0)
             high = prob.astype(BF16)
             left += [keys[number], keys[number]]
             right += [high, (prob - high.astype(F32)).astype(BF16)]
-        means = means + lax.dot_general(
+        fade = jnp.concatenate([jnp.broadcast_to(row, (HALF, queries)) for row in fades], axis=0)
+        means = means * fade + lax.dot_general(
             jnp.concatenate(left, axis=0),
             jnp.concatenate(right, axis=0),
             (((0,), (0,)), ((), ())),
             preferred_element_type=F32,
         )
-        return sums[0], sums[1], means
-
+        return *tops, *sums, means
+
+    lowest = jnp.full((1, queries), -1e30, F32)
     none = jnp.zeros((8, queries), F32)
-    state = lax.fori_loop(
-        0, steps, gather, (none, none, jnp.zeros((LANES, queries), F32)), unroll=True
-    )
+    state = (lowest, lowest, none, none, jnp.zeros((LANES, queries), F32))
+    state = lax.fori_loop(0, keys_ref.shape[0] // chunk, step, state, unroll=True)
+    tops, state = state[:2], state[2:]
     lines, columns = [], []
     for kind in range(2):
         total = jnp.sum(state[kind], axis=0, keepdims=True)
@@ -356,9 +356,8 @@
 
     deep = queries // groups
     logs, spans = call(
-        functools.partial(totals_kernel, 8, 32),
+        functools.partial(totals_kernel, 8),
         (shape((groups, 3 * deep // 4 + 8, LANES), F32), shape((3, queries, LANES), BF16)),
-        scratch=[pltpu.VMEM((4, heads * half, queries), F32)],
         smem=1,
         flops=2**31,
     )(spot, keys, rows)

time: 107 us -> 107 us (level)
  no operation moved by 1% of the time
where the time goes in v6:
time: 107 us
  starting transfers between devices  39.6 us (37%)
  blocking collectives  33.3 us (31%)
  waiting for transfers between devices  19.3 us (18%)
  Pallas kernels  13.1 us (12%)
    all_gather x1, blocking collectives, on_device(): lax.all_gather(shard, ('group', 'near', 'core'), axis=0, tiled=True, axis...  33.3 us
    all_to_all x2, starting transfers between devices, trade(): return lax.all_to_all(array, axes, split_axis=0, concat_axis=0, tiled=True)  24.6 us
    all_to_all x1, waiting for transfers between devices, on_device(): lax.all_to_all(logs, ('group', 'near', 'core'), split_axis=0, concat_axis...  15.2 us
    pallas_call x5, Pallas kernels, run(): pl.pallas_call(body, out_shape=shapes, in_specs=specs((smem, raw, len(arg...  13.1 us
    all_to_all x1, starting transfers between devices, on_device(): lax.all_to_all(logs, ('group', 'near', 'core'), split_axis=0, concat_axis...  6.34 us
    ppermute x2, starting transfers between devices, on_device(): flip = lambda array, axis: lax.ppermute(array, axis, [(0, 1), (1, 0)])  6.13 us
    ppermute x2, waiting for transfers between devices, on_device(): flip = lambda array, axis: lax.ppermute(array, axis, [(0, 1), (1, 0)])  2.65 us
    ppermute x1, starting transfers between devices, on_device(): other = lax.ppermute(given, 'core', [(0, 1), (1, 0)])  2.48 us
  transfers between devices with their start and end apart: 6, of which 5 were waited for; matrix products, arithmetic and copies ran while one was open for 0% of the time, Pallas kernels for 1%

profile of v6, /device:TPU:1, one launch (start us, length us, event | category | flops | bytes accessed | tf_op | source)
XLA Modules:
  0.0 107.0 jit_solution(3139360465273624636)
XLA Ops:
  0.6 2.8 %shard_map.68 = (bf16[64,48,128]{2,1,0:T(8,128)(2,1)}, bf16[48,128]{1,0:T(8,128)(2,1)}, bf16[48,128]{1,0:T(8,128)(2,1)}) custom-call(s32[1]{0:T(128)S(6)} %xor.7.side_ref, s32[1]{0:T(128)} %bitcast.2.turn_ref, bf16[16,512]{1,0:T(8,128)(2,1)} %tq_hbm.1, bf16[32,8192]{1,0:T(8,128)(2,1)} %tk_hbm.1, bf16[16,160]{1,0:T(8,128)(2,1)} %sq_hbm.1, bf16[32,2560]{1,0:T(8,128)(2,1)} %sk_hbm.1), custom_call_target="tpu_custom_call" | custom-call | bytes 709640 | tf_op jit(solution)/shard_map/pallas_call | solution.py:283
  3.4 0.0 copy-start.2
  3.5 0.0 copy-start
  3.5 11.0 %all-to-all-start = ((bf16[64,48,128]{2,1,0:T(8,128)(2,1)}), bf16[64,48,128]{2,1,0:T(8,128)(2,1)S(1)}, u32[]{:S(2)}, u32[]{:S(2)}) async-start(bf16[64,48,128]{2,1,0:T(8,128)(2,1)} %get-tuple-element.9), calls=%async_computation | async-start | bytes 1572864 | tf_op jit(solution)/shard_map/all_to_all | solution.py:310
  14.4 0.0 copy-done.2
  14.5 2.5 %collective-permute-start = (bf16[48,128]{1,0:T(8,128)(2,1)S(1)}, bf16[48,128]{1,0:T(8,128)(2,1)S(1)}, u32[]{:S(2)}, u32[]{:S(2)}) collective-permute-start(bf16[48,128]{1,0:T(8,128)(2,1)S(1)} %copy-done.2), channel_id=1, source_target_pairs={{0,16},{16,0},{1,17},{17,1},{2,18},{18,2},{3,19},{19,3},{4,20},{20... | collective-permute-start | bytes 36872 | tf_op jit(solution)/shard_map/ppermute | solution.py:340
  16.9 0.8 collective-permute-done
  17.7 0.0 copy-done
  17.8 33.3 %all_gather.3.rows_ref = bf16[16,96,128]{2,1,0:T(8,128)(2,1)S(1)} all-gather(bf16[1,96,128]{2,1,0:T(8,128)(2,1)S(1)} %bitcast.8), channel_id=1, replica_groups={{0,48,80,96,128,176,208,224,256,304,336,352,384,432,464,480},{16,32,64,..., dimensions={0}, use_global_device_ids=true | all-gather | bytes 417792 | tf_op jit(solution)/shard_map/all_gather | solution.py:347
  51.1 0.0 all-to-all-done.keys_ref
  51.1 5.7 %shard_map.69 = (f32[8,56,128]{2,1,0:T(8,128)}, bf16[3,512,128]{2,1,0:T(8,128)(2,1)S(1)}) custom-call(s32[1]{0:T(128)} %bitcast.near_ref, bf16[64,48,128]{2,1,0:T(8,128)(2,1)S(1)} %all-to-all-done.keys_ref, bf16[16,96,128]{2,1,0:T(8,128)(2,1)S(1)} %all_gather.3.rows_ref), custom_call_target="tpu_custom_call" | custom-call | flops 2147483648 | bytes 1179652 | tf_op jit(solution)/shard_map/pallas_call | solution.py:283
  56.8 6.3 %all-to-all-start.1 = ((f32[8,56,128]{2,1,0:T(8,128)}), f32[8,56,128]{2,1,0:T(8,128)S(1)}, u32[]{:S(2)}, u32[]{:S(2)}) async-start(f32[8,56,128]{2,1,0:T(8,128)} %get-tuple-element.12), calls=%async_computation.1 | async-start | bytes 458752 | tf_op jit(solution)/shard_map/all_to_all | solution.py:364
  63.2 0.0 copy-start.1
  63.2 0.7 copy-done.1
  63.9 0.1 dynamic_slice.3
  63.9 15.2 %all-to-all-done.1.logs_ref = f32[8,56,128]{2,1,0:T(8,128)S(1)} async-done(((f32[8,56,128]{2,1,0:T(8,128)}), f32[8,56,128]{2,1,0:T(8,128)S(1)}, u32[]{:S(2)}, u32[]{:S(2)}) %all-to-all-start.1) | async-done | bytes 229408 | tf_op jit(solution)/shard_map/all_to_all | solution.py:364
  79.1 0.1 broadcast_in_dim.2.own_ref
  79.2 3.0 %shard_map.70 = (bf16[64,16,128]{2,1,0:T(8,128)(2,1)}, f32[4,16,128]{2,1,0:T(8,128)S(1)}) custom-call(s32[1]{0:T(128)} %bitcast.near_ref, s32[1]{0:T(128)} %bitcast.1.core_ref, f32[8,56,128]{2,1,0:T(8,128)S(1)} %all-to-all-done.1.logs_ref, f32[1,512]{1,0:T(1,128)S(1)} %bitcast.7, f32[64,128]{1,0:T(8,128)S(1)} %broadcast_in_dim.2.own_ref, ...), custom_call_target="tpu_custom_call" | custom-call | flops 1073741824 | bytes 1443848 | tf_op jit(solution)/shard_map/pallas_call | solution.py:283
  82.2 13.7 %all-to-all-start.2 = ((bf16[64,16,128]{2,1,0:T(8,128)(2,1)}), bf16[64,16,128]{2,1,0:T(8,128)(2,1)S(1)}, u32[]{:S(2)}, u32[]{:S(2)}) async-start(bf16[64,16,128]{2,1,0:T(8,128)(2,1)} %get-tuple-element.15), calls=%async_computation.2 | async-start | bytes 524288 | tf_op jit(solution)/shard_map/all_to_all | solution.py:310
  95.9 3.3 %collective-permute-start.1 = (f32[2,16,128]{2,1,0:T(8,128)S(1)}, f32[2,16,128]{2,1,0:T(8,128)S(1)}, u32[]{:S(2)}, u32[]{:S(2)}) collective-permute-start(f32[2,16,128]{2,1,0:T(8,128)S(1)} %slice.9), channel_id=1, source_target_pairs={{0,32},{32,0},{1,33},{33,1},{2,34},{34,2},{3,35},{35,3},{4,36},{36... | collective-permute-start | bytes 49160 | tf_op jit(solution)/shard_map/ppermute | solution.py:388
  99.2 1.8 %collective-permute-done.1.along_ref = f32[2,16,128]{2,1,0:T(8,128)S(1)} collective-permute-done((f32[2,16,128]{2,1,0:T(8,128)S(1)}, f32[2,16,128]{2,1,0:T(8,128)S(1)}, u32[]{:S(2)}, u32[]{:S(2)}) %collective-permute-start.1) | collective-permute-done | bytes 16416 | tf_op jit(solution)/shard_map/ppermute | solution.py:388
  101.0 2.8 %collective-permute-start.2 = (f32[2,16,128]{2,1,0:T(8,128)S(1)}, f32[2,16,128]{2,1,0:T(8,128)S(1)}, u32[]{:S(2)}, u32[]{:S(2)}) collective-permute-start(f32[2,16,128]{2,1,0:T(8,128)S(1)} %pad_maximum_fusion), channel_id=1, source_target_pairs={{0,16},{16,0},{1,17},{17,1},{2,18},{18,2},{3,19},{19,3},{4,20},{20... | collective-permute-start | bytes 49160 | tf_op jit(solution)/shard_map/ppermute | solution.py:388
  103.9 0.8 collective-permute-done.2.across_ref
  104.7 0.7 shard_map.71
  105.4 0.6 all-to-all-done.2.in_ref
  106.0 0.9 shard_map.72
  (7 shorter events, 0.0 us)
Async XLA Ops:
  3.4 11.0 %copy-start.2 = (bf16[48,128]{1,0:T(8,128)(2,1)S(1)}, bf16[48,128]{1,0:T(8,128)(2,1)}, u32[]{:S(2)}) copy-start(bf16[48,128]{1,0:T(8,128)(2,1)} %get-tuple-element.11) | copy-start | bytes 36868
  3.5 14.3 %copy-start = (bf16[48,128]{1,0:T(8,128)(2,1)S(1)}, bf16[48,128]{1,0:T(8,128)(2,1)}, u32[]{:S(2)}) copy-start(bf16[48,128]{1,0:T(8,128)(2,1)} %get-tuple-element.10) | copy-start | bytes 36868
  3.5 47.6 %all-to-all-start = ((bf16[64,48,128]{2,1,0:T(8,128)(2,1)}), bf16[64,48,128]{2,1,0:T(8,128)(2,1)S(1)}, u32[]{:S(2)}, u32[]{:S(2)}) async-start(bf16[64,48,128]{2,1,0:T(8,128)(2,1)} %get-tuple-element.9), calls=%async_computation | async-start | bytes 1572864 | tf_op jit(solution)/shard_map/all_to_all | solution.py:310
  14.5 3.3 %collective-permute-start = (bf16[48,128]{1,0:T(8,128)(2,1)S(1)}, bf16[48,128]{1,0:T(8,128)(2,1)S(1)}, u32[]{:S(2)}, u32[]{:S(2)}) collective-permute-start(bf16[48,128]{1,0:T(8,128)(2,1)S(1)} %copy-done.2), channel_id=1, source_target_pairs={{0,16},{16,0},{1,17},{17,1},{2,18},{18,2},{3,19},{19,3},{4,20},{20... | collective-permute-start | bytes 36872 | tf_op jit(solution)/shard_map/ppermute | solution.py:340
  56.8 22.3 %all-to-all-start.1 = ((f32[8,56,128]{2,1,0:T(8,128)}), f32[8,56,128]{2,1,0:T(8,128)S(1)}, u32[]{:S(2)}, u32[]{:S(2)}) async-start(f32[8,56,128]{2,1,0:T(8,128)} %get-tuple-element.12), calls=%async_computation.1 | async-start | bytes 458752 | tf_op jit(solution)/shard_map/all_to_all | solution.py:364
  63.2 0.7 copy-start.1
  82.2 23.9 %all-to-all-start.2 = ((bf16[64,16,128]{2,1,0:T(8,128)(2,1)}), bf16[64,16,128]{2,1,0:T(8,128)(2,1)S(1)}, u32[]{:S(2)}, u32[]{:S(2)}) async-start(bf16[64,16,128]{2,1,0:T(8,128)(2,1)} %get-tuple-element.15), calls=%async_computation.2 | async-start | bytes 524288 | tf_op jit(solution)/shard_map/all_to_all | solution.py:310
  95.9 5.1 %collective-permute-start.1 = (f32[2,16,128]{2,1,0:T(8,128)S(1)}, f32[2,16,128]{2,1,0:T(8,128)S(1)}, u32[]{:S(2)}, u32[]{:S(2)}) collective-permute-start(f32[2,16,128]{2,1,0:T(8,128)S(1)} %slice.9), channel_id=1, source_target_pairs={{0,32},{32,0},{1,33},{33,1},{2,34},{34,2},{3,35},{35,3},{4,36},{36... | collective-permute-start | bytes 49160 | tf_op jit(solution)/shard_map/ppermute | solution.py:388
  101.0 3.7 %collective-permute-start.2 = (f32[2,16,128]{2,1,0:T(8,128)S(1)}, f32[2,16,128]{2,1,0:T(8,128)S(1)}, u32[]{:S(2)}, u32[]{:S(2)}) collective-permute-start(f32[2,16,128]{2,1,0:T(8,128)S(1)} %pad_maximum_fusion), channel_id=1, source_target_pairs={{0,16},{16,0},{1,17},{17,1},{2,18},{18,2},{3,19},{19,3},{4,20},{20... | collective-permute-start | bytes 49160 | tf_op jit(solution)/shard_map/ppermute | solution.py:388

commit v7 on v5

--- a/solution.py
+++ b/solution.py
@@ -356,7 +356,7 @@
 
     deep = queries // groups
     logs, spans = call(
-        functools.partial(totals_kernel, 8, 32),
+        functools.partial(totals_kernel, 16, 32),
         (shape((groups, 3 * deep // 4 + 8, LANES), F32), shape((3, queries, LANES), BF16)),
         scratch=[pltpu.VMEM((4, heads * half, queries), F32)],
         smem=1,

time: 107 us -> 107 us (level)
  no operation moved by 1% of the time
where the time goes in v7:
time: 107 us
  starting transfers between devices  39.6 us (37%)
  blocking collectives  33.3 us (31%)
  waiting for transfers between devices  19.3 us (18%)
  Pallas kernels  12.8 us (12%)
    all_gather x1, blocking collectives, on_device(): lax.all_gather(shard, ('group', 'near', 'core'), axis=0, tiled=True, axis...  33.3 us
    all_to_all x2, starting transfers between devices, trade(): return lax.all_to_all(array, axes, split_axis=0, concat_axis=0, tiled=True)  24.6 us
    all_to_all x1, waiting for transfers between devices, on_device(): lax.all_to_all(logs, ('group', 'near', 'core'), split_axis=0, concat_axis...  15.2 us
    pallas_call x5, Pallas kernels, run(): pl.pallas_call(body, out_shape=shapes, in_specs=specs((smem, raw, len(arg...  12.8 us
    all_to_all x1, starting transfers between devices, on_device(): lax.all_to_all(logs, ('group', 'near', 'core'), split_axis=0, concat_axis...  6.35 us
    ppermute x2, starting transfers between devices, on_device(): flip = lambda array, axis: lax.ppermute(array, axis, [(0, 1), (1, 0)])  6.13 us
    ppermute x2, waiting for transfers between devices, on_device(): flip = lambda array, axis: lax.ppermute(array, axis, [(0, 1), (1, 0)])  2.65 us
    ppermute x1, starting transfers between devices, on_device(): other = lax.ppermute(given, 'core', [(0, 1), (1, 0)])  2.48 us
  transfers between devices with their start and end apart: 6, of which 5 were waited for; matrix products, arithmetic and copies ran while one was open for 0% of the time, Pallas kernels for 1%

profile of v7, /device:TPU:1, one launch (start us, length us, event | category | flops | bytes accessed | tf_op | source)
XLA Modules:
  0.0 106.6 jit_solution(5404824676173423353)
XLA Ops:
  0.6 2.8 %shard_map.68 = (bf16[64,48,128]{2,1,0:T(8,128)(2,1)}, bf16[48,128]{1,0:T(8,128)(2,1)}, bf16[48,128]{1,0:T(8,128)(2,1)}) custom-call(s32[1]{0:T(128)S(6)} %xor.7.side_ref, s32[1]{0:T(128)} %bitcast.2.turn_ref, bf16[16,512]{1,0:T(8,128)(2,1)} %tq_hbm.1, bf16[32,8192]{1,0:T(8,128)(2,1)} %tk_hbm.1, bf16[16,160]{1,0:T(8,128)(2,1)} %sq_hbm.1, bf16[32,2560]{1,0:T(8,128)(2,1)} %sk_hbm.1), custom_call_target="tpu_custom_call" | custom-call | bytes 709640 | tf_op jit(solution)/shard_map/pallas_call | solution.py:283
  3.4 0.0 copy-start.2
  3.5 0.0 copy-start
  3.5 11.0 %all-to-all-start = ((bf16[64,48,128]{2,1,0:T(8,128)(2,1)}), bf16[64,48,128]{2,1,0:T(8,128)(2,1)S(1)}, u32[]{:S(2)}, u32[]{:S(2)}) async-start(bf16[64,48,128]{2,1,0:T(8,128)(2,1)} %get-tuple-element.9), calls=%async_computation | async-start | bytes 1572864 | tf_op jit(solution)/shard_map/all_to_all | solution.py:310
  14.4 0.0 copy-done.2
  14.5 2.5 %collective-permute-start = (bf16[48,128]{1,0:T(8,128)(2,1)S(1)}, bf16[48,128]{1,0:T(8,128)(2,1)S(1)}, u32[]{:S(2)}, u32[]{:S(2)}) collective-permute-start(bf16[48,128]{1,0:T(8,128)(2,1)S(1)} %copy-done.2), channel_id=1, source_target_pairs={{0,16},{16,0},{1,17},{17,1},{2,18},{18,2},{3,19},{19,3},{4,20},{20... | collective-permute-start | bytes 36872 | tf_op jit(solution)/shard_map/ppermute | solution.py:340
  16.9 0.8 collective-permute-done
  17.7 0.0 copy-done
  17.8 33.3 %all_gather.3.rows_ref = bf16[16,96,128]{2,1,0:T(8,128)(2,1)S(1)} all-gather(bf16[1,96,128]{2,1,0:T(8,128)(2,1)S(1)} %bitcast.8), channel_id=1, replica_groups={{0,48,80,96,128,176,208,224,256,304,336,352,384,432,464,480},{16,32,64,..., dimensions={0}, use_global_device_ids=true | all-gather | bytes 417792 | tf_op jit(solution)/shard_map/all_gather | solution.py:347
  51.1 0.0 all-to-all-done.keys_ref
  51.1 5.4 %shard_map.69 = (f32[8,56,128]{2,1,0:T(8,128)}, bf16[3,512,128]{2,1,0:T(8,128)(2,1)S(1)}) custom-call(s32[1]{0:T(128)} %bitcast.near_ref, bf16[64,48,128]{2,1,0:T(8,128)(2,1)S(1)} %all-to-all-done.keys_ref, bf16[16,96,128]{2,1,0:T(8,128)(2,1)S(1)} %all_gather.3.rows_ref), custom_call_target="tpu_custom_call" | custom-call | flops 2147483648 | bytes 1179652 | tf_op jit(solution)/shard_map/pallas_call | solution.py:283
  56.5 6.3 %all-to-all-start.1 = ((f32[8,56,128]{2,1,0:T(8,128)}), f32[8,56,128]{2,1,0:T(8,128)S(1)}, u32[]{:S(2)}, u32[]{:S(2)}) async-start(f32[8,56,128]{2,1,0:T(8,128)} %get-tuple-element.12), calls=%async_computation.1 | async-start | bytes 458752 | tf_op jit(solution)/shard_map/all_to_all | solution.py:365
  62.8 0.0 copy-start.1
  62.8 0.7 copy-done.1
  63.5 0.1 dynamic_slice.3
  63.6 15.2 %all-to-all-done.1.logs_ref = f32[8,56,128]{2,1,0:T(8,128)S(1)} async-done(((f32[8,56,128]{2,1,0:T(8,128)}), f32[8,56,128]{2,1,0:T(8,128)S(1)}, u32[]{:S(2)}, u32[]{:S(2)}) %all-to-all-start.1) | async-done | bytes 229408 | tf_op jit(solution)/shard_map/all_to_all | solution.py:365
  78.8 0.1 broadcast_in_dim.2.own_ref
  78.8 3.0 %shard_map.70 = (bf16[64,16,128]{2,1,0:T(8,128)(2,1)}, f32[4,16,128]{2,1,0:T(8,128)S(1)}) custom-call(s32[1]{0:T(128)} %bitcast.near_ref, s32[1]{0:T(128)} %bitcast.1.core_ref, f32[8,56,128]{2,1,0:T(8,128)S(1)} %all-to-all-done.1.logs_ref, f32[1,512]{1,0:T(1,128)S(1)} %bitcast.7, f32[64,128]{1,0:T(8,128)S(1)} %broadcast_in_dim.2.own_ref, ...), custom_call_target="tpu_custom_call" | custom-call | flops 1073741824 | bytes 1443848 | tf_op jit(solution)/shard_map/pallas_call | solution.py:283
  81.8 13.6 %all-to-all-start.2 = ((bf16[64,16,128]{2,1,0:T(8,128)(2,1)}), bf16[64,16,128]{2,1,0:T(8,128)(2,1)S(1)}, u32[]{:S(2)}, u32[]{:S(2)}) async-start(bf16[64,16,128]{2,1,0:T(8,128)(2,1)} %get-tuple-element.15), calls=%async_computation.2 | async-start | bytes 524288 | tf_op jit(solution)/shard_map/all_to_all | solution.py:310
  95.5 3.3 %collective-permute-start.1 = (f32[2,16,128]{2,1,0:T(8,128)S(1)}, f32[2,16,128]{2,1,0:T(8,128)S(1)}, u32[]{:S(2)}, u32[]{:S(2)}) collective-permute-start(f32[2,16,128]{2,1,0:T(8,128)S(1)} %slice.9), channel_id=1, source_target_pairs={{0,32},{32,0},{1,33},{33,1},{2,34},{34,2},{3,35},{35,3},{4,36},{36... | collective-permute-start | bytes 49160 | tf_op jit(solution)/shard_map/ppermute | solution.py:389
  98.8 1.8 %collective-permute-done.1.along_ref = f32[2,16,128]{2,1,0:T(8,128)S(1)} collective-permute-done((f32[2,16,128]{2,1,0:T(8,128)S(1)}, f32[2,16,128]{2,1,0:T(8,128)S(1)}, u32[]{:S(2)}, u32[]{:S(2)}) %collective-permute-start.1) | collective-permute-done | bytes 16416 | tf_op jit(solution)/shard_map/ppermute | solution.py:389
  100.7 2.8 %collective-permute-start.2 = (f32[2,16,128]{2,1,0:T(8,128)S(1)}, f32[2,16,128]{2,1,0:T(8,128)S(1)}, u32[]{:S(2)}, u32[]{:S(2)}) collective-permute-start(f32[2,16,128]{2,1,0:T(8,128)S(1)} %pad_maximum_fusion), channel_id=1, source_target_pairs={{0,16},{16,0},{1,17},{17,1},{2,18},{18,2},{3,19},{19,3},{4,20},{20... | collective-permute-start | bytes 49160 | tf_op jit(solution)/shard_map/ppermute | solution.py:389
  103.5 0.8 collective-permute-done.2.across_ref
  104.3 0.7 shard_map.71
  105.0 0.6 all-to-all-done.2.in_ref
  105.7 0.9 shard_map.72
  (7 shorter events, 0.0 us)
Async XLA Ops:
  3.4 11.0 %copy-start.2 = (bf16[48,128]{1,0:T(8,128)(2,1)S(1)}, bf16[48,128]{1,0:T(8,128)(2,1)}, u32[]{:S(2)}) copy-start(bf16[48,128]{1,0:T(8,128)(2,1)} %get-tuple-element.11) | copy-start | bytes 36868
  3.5 14.3 %copy-start = (bf16[48,128]{1,0:T(8,128)(2,1)S(1)}, bf16[48,128]{1,0:T(8,128)(2,1)}, u32[]{:S(2)}) copy-start(bf16[48,128]{1,0:T(8,128)(2,1)} %get-tuple-element.10) | copy-start | bytes 36868
  3.5 47.6 %all-to-all-start = ((bf16[64,48,128]{2,1,0:T(8,128)(2,1)}), bf16[64,48,128]{2,1,0:T(8,128)(2,1)S(1)}, u32[]{:S(2)}, u32[]{:S(2)}) async-start(bf16[64,48,128]{2,1,0:T(8,128)(2,1)} %get-tuple-element.9), calls=%async_computation | async-start | bytes 1572864 | tf_op jit(solution)/shard_map/all_to_all | solution.py:310
  14.5 3.3 %collective-permute-start = (bf16[48,128]{1,0:T(8,128)(2,1)S(1)}, bf16[48,128]{1,0:T(8,128)(2,1)S(1)}, u32[]{:S(2)}, u32[]{:S(2)}) collective-permute-start(bf16[48,128]{1,0:T(8,128)(2,1)S(1)} %copy-done.2), channel_id=1, source_target_pairs={{0,16},{16,0},{1,17},{17,1},{2,18},{18,2},{3,19},{19,3},{4,20},{20... | collective-permute-start | bytes 36872 | tf_op jit(solution)/shard_map/ppermute | solution.py:340
  56.5 22.3 %all-to-all-start.1 = ((f32[8,56,128]{2,1,0:T(8,128)}), f32[8,56,128]{2,1,0:T(8,128)S(1)}, u32[]{:S(2)}, u32[]{:S(2)}) async-start(f32[8,56,128]{2,1,0:T(8,128)} %get-tuple-element.12), calls=%async_computation.1 | async-start | bytes 458752 | tf_op jit(solution)/shard_map/all_to_all | solution.py:365
  62.8 0.7 copy-start.1
  81.8 23.8 %all-to-all-start.2 = ((bf16[64,16,128]{2,1,0:T(8,128)(2,1)}), bf16[64,16,128]{2,1,0:T(8,128)(2,1)S(1)}, u32[]{:S(2)}, u32[]{:S(2)}) async-start(bf16[64,16,128]{2,1,0:T(8,128)(2,1)} %get-tuple-element.15), calls=%async_computation.2 | async-start | bytes 524288 | tf_op jit(solution)/shard_map/all_to_all | solution.py:310
  95.5 5.1 %collective-permute-start.1 = (f32[2,16,128]{2,1,0:T(8,128)S(1)}, f32[2,16,128]{2,1,0:T(8,128)S(1)}, u32[]{:S(2)}, u32[]{:S(2)}) collective-permute-start(f32[2,16,128]{2,1,0:T(8,128)S(1)} %slice.9), channel_id=1, source_target_pairs={{0,32},{32,0},{1,33},{33,1},{2,34},{34,2},{3,35},{35,3},{4,36},{36... | collective-permute-start | bytes 49160 | tf_op jit(solution)/shard_map/ppermute | solution.py:389
  100.7 3.7 %collective-permute-start.2 = (f32[2,16,128]{2,1,0:T(8,128)S(1)}, f32[2,16,128]{2,1,0:T(8,128)S(1)}, u32[]{:S(2)}, u32[]{:S(2)}) collective-permute-start(f32[2,16,128]{2,1,0:T(8,128)S(1)} %pad_maximum_fusion), channel_id=1, source_target_pairs={{0,16},{16,0},{1,17},{17,1},{2,18},{18,2},{3,19},{19,3},{4,20},{20... | collective-permute-start | bytes 49160 | tf_op jit(solution)/shard_map/ppermute | solution.py:389

commit v8 on v4

--- a/solution.py
+++ b/solution.py
@@ -362,7 +362,7 @@
     own = lax.dynamic_slice(weights, (lax.axis_index("group") * deep,), (deep,))
     own = jnp.broadcast_to(own[:, None], (deep, LANES))
     parts, mine = call(
-        functools.partial(grads_kernel, 8),
+        functools.partial(grads_kernel, 32),
         (shape((heads, half, LANES), BF16), shape((near, rows_own, LANES), F32)),
         scratch=[pltpu.VMEM((near, rows_own, LANES), F32)],
         smem=2,

time: 108 us -> 107 us (level)
  no operation moved by 1% of the time
where the time goes in v8:
time: 107 us; the launch traced here: 106 us
  starting transfers between devices  36.4 us (34%)
  blocking collectives  34.7 us (32%)
  waiting for transfers between devices  21 us (20%)
  Pallas kernels  12.8 us (12%)
    all_gather x1, blocking collectives, on_device(): lax.all_gather(shard, ('group', 'near', 'core'), axis=0, tiled=True, axis...  34.7 us
    all_to_all x3, starting transfers between devices, trade(): return lax.all_to_all(array, axes, split_axis=0, concat_axis=0, tiled=True)  27.8 us
    all_to_all x3, waiting for transfers between devices, trade(): return lax.all_to_all(array, axes, split_axis=0, concat_axis=0, tiled=True)  17.5 us
    pallas_call x5, Pallas kernels, run(): pl.pallas_call(body, out_shape=shapes, in_specs=specs((smem, raw, len(arg...  12.8 us
    ppermute x2, starting transfers between devices, on_device(): flip = lambda array, axis: lax.ppermute(array, axis, [(0, 1), (1, 0)])  6.13 us
    ppermute x2, waiting for transfers between devices, on_device(): flip = lambda array, axis: lax.ppermute(array, axis, [(0, 1), (1, 0)])  2.65 us
    ppermute x1, starting transfers between devices, on_device(): other = lax.ppermute(given, 'core', [(0, 1), (1, 0)])  2.48 us
  transfers between devices with their start and end apart: 6, of which 5 were waited for; matrix products, arithmetic and copies ran while one was open for 0% of the time, Pallas kernels for 1%

profile of v8, /device:TPU:1, one launch (start us, length us, event | category | flops | bytes accessed | tf_op | source)
XLA Modules:
  0.0 106.5 jit_solution(12874130103307244867)
XLA Ops:
  0.6 2.8 %shard_map.68 = (bf16[64,48,128]{2,1,0:T(8,128)(2,1)}, bf16[48,128]{1,0:T(8,128)(2,1)}, bf16[48,128]{1,0:T(8,128)(2,1)}) custom-call(s32[1]{0:T(128)S(6)} %xor.3.side_ref, bf16[16,512]{1,0:T(8,128)(2,1)} %tq_hbm.1, bf16[32,8192]{1,0:T(8,128)(2,1)} %tk_hbm.1, bf16[16,160]{1,0:T(8,128)(2,1)} %sq_hbm.1, bf16[32,2560]{1,0:T(8,128)(2,1)} %sk_hbm.1), custom_call_target="tpu_custom_call" | custom-call | bytes 709636 | tf_op jit(solution)/shard_map/pallas_call | solution.py:283
  3.4 0.0 copy-start.2
  3.4 0.0 copy-start
  3.5 11.0 %all-to-all-start = ((bf16[64,48,128]{2,1,0:T(8,128)(2,1)}), bf16[64,48,128]{2,1,0:T(8,128)(2,1)S(1)}, u32[]{:S(2)}, u32[]{:S(2)}) async-start(bf16[64,48,128]{2,1,0:T(8,128)(2,1)} %get-tuple-element.9), calls=%async_computation | async-start | bytes 1572864 | tf_op jit(solution)/shard_map/all_to_all | solution.py:306
  14.4 0.0 copy-done.2
  14.4 2.5 %collective-permute-start = (bf16[48,128]{1,0:T(8,128)(2,1)S(1)}, bf16[48,128]{1,0:T(8,128)(2,1)S(1)}, u32[]{:S(2)}, u32[]{:S(2)}) collective-permute-start(bf16[48,128]{1,0:T(8,128)(2,1)S(1)} %copy-done.2), channel_id=1, source_target_pairs={{0,16},{16,0},{1,17},{17,1},{2,18},{18,2},{3,19},{19,3},{4,20},{20... | collective-permute-start | bytes 36872 | tf_op jit(solution)/shard_map/ppermute | solution.py:334
  16.9 0.8 collective-permute-done
  17.7 0.0 copy-done
  17.8 34.7 %all_gather.3.rows_ref = bf16[16,96,128]{2,1,0:T(8,128)(2,1)S(1)} all-gather(bf16[1,96,128]{2,1,0:T(8,128)(2,1)S(1)} %bitcast.7), channel_id=1, replica_groups={{0,48,64,112,128,176,192,240,256,304,320,368,384,432,448,496},{16,32,80..., dimensions={0}, use_global_device_ids=true | all-gather | bytes 417792 | tf_op jit(solution)/shard_map/all_gather | solution.py:341
  52.4 0.0 all-to-all-done.keys_ref
  52.5 5.4 %shard_map.69 = (f32[8,56,128]{2,1,0:T(8,128)}, bf16[3,512,128]{2,1,0:T(8,128)(2,1)S(1)}) custom-call(s32[1]{0:T(128)} %bitcast.near_ref, bf16[64,48,128]{2,1,0:T(8,128)(2,1)S(1)} %all-to-all-done.keys_ref, bf16[16,96,128]{2,1,0:T(8,128)(2,1)S(1)} %all_gather.3.rows_ref), custom_call_target="tpu_custom_call" | custom-call | flops 2147483648 | bytes 1179652 | tf_op jit(solution)/shard_map/pallas_call | solution.py:283
  57.8 6.5 %all-to-all-start.1 = ((f32[8,56,128]{2,1,0:T(8,128)}), f32[8,56,128]{2,1,0:T(8,128)S(1)}, u32[]{:S(2)}, u32[]{:S(2)}) async-start(f32[8,56,128]{2,1,0:T(8,128)} %get-tuple-element.12), calls=%async_computation.1 | async-start | bytes 458752 | tf_op jit(solution)/shard_map/all_to_all | solution.py:306
  64.3 0.0 copy-start.1
  64.3 0.7 copy-done.1
  65.0 0.1 dynamic_slice.3
  65.1 16.9 %all-to-all-done.1.logs_ref = f32[8,56,128]{2,1,0:T(8,128)S(1)} async-done(((f32[8,56,128]{2,1,0:T(8,128)}), f32[8,56,128]{2,1,0:T(8,128)S(1)}, u32[]{:S(2)}, u32[]{:S(2)}) %all-to-all-start.1) | async-done | bytes 229408 | tf_op jit(solution)/shard_map/all_to_all | solution.py:306
  82.0 0.1 broadcast_in_dim.2.own_ref
  82.0 3.0 %shard_map.70 = (bf16[64,16,128]{2,1,0:T(8,128)(2,1)}, f32[4,16,128]{2,1,0:T(8,128)S(1)}) custom-call(s32[1]{0:T(128)} %bitcast.near_ref, s32[1]{0:T(128)} %bitcast.1.core_ref, f32[8,56,128]{2,1,0:T(8,128)S(1)} %all-to-all-done.1.logs_ref, f32[1,512]{1,0:T(1,128)S(1)} %bitcast.6, f32[64,128]{1,0:T(8,128)S(1)} %broadcast_in_dim.2.own_ref, ...), custom_call_target="tpu_custom_call" | custom-call | flops 1073741824 | bytes 1443848 | tf_op jit(solution)/shard_map/pallas_call | solution.py:283
  85.1 10.3 %all-to-all-start.2 = ((bf16[64,16,128]{2,1,0:T(8,128)(2,1)}), bf16[64,16,128]{2,1,0:T(8,128)(2,1)S(1)}, u32[]{:S(2)}, u32[]{:S(2)}) async-start(bf16[64,16,128]{2,1,0:T(8,128)(2,1)} %get-tuple-element.15), calls=%async_computation.2 | async-start | bytes 524288 | tf_op jit(solution)/shard_map/all_to_all | solution.py:306
  95.4 3.3 %collective-permute-start.1 = (f32[2,16,128]{2,1,0:T(8,128)S(1)}, f32[2,16,128]{2,1,0:T(8,128)S(1)}, u32[]{:S(2)}, u32[]{:S(2)}) collective-permute-start(f32[2,16,128]{2,1,0:T(8,128)S(1)} %slice.9), channel_id=1, source_target_pairs={{0,32},{32,0},{1,33},{33,1},{2,34},{34,2},{3,35},{35,3},{4,36},{36... | collective-permute-start | bytes 49160 | tf_op jit(solution)/shard_map/ppermute | solution.py:372
  98.7 1.8 %collective-permute-done.1.along_ref = f32[2,16,128]{2,1,0:T(8,128)S(1)} collective-permute-done((f32[2,16,128]{2,1,0:T(8,128)S(1)}, f32[2,16,128]{2,1,0:T(8,128)S(1)}, u32[]{:S(2)}, u32[]{:S(2)}) %collective-permute-start.1) | collective-permute-done | bytes 16416 | tf_op jit(solution)/shard_map/ppermute | solution.py:372
  100.5 2.8 %collective-permute-start.2 = (f32[2,16,128]{2,1,0:T(8,128)S(1)}, f32[2,16,128]{2,1,0:T(8,128)S(1)}, u32[]{:S(2)}, u32[]{:S(2)}) collective-permute-start(f32[2,16,128]{2,1,0:T(8,128)S(1)} %pad_maximum_fusion), channel_id=1, source_target_pairs={{0,16},{16,0},{1,17},{17,1},{2,18},{18,2},{3,19},{19,3},{4,20},{20... | collective-permute-start | bytes 49160 | tf_op jit(solution)/shard_map/ppermute | solution.py:372
  103.4 0.8 collective-permute-done.2.across_ref
  104.2 0.7 shard_map.71
  104.9 0.6 all-to-all-done.2.in_ref
  105.5 0.9 shard_map.72
  (7 shorter events, 0.0 us)
Async XLA Ops:
  3.4 11.0 %copy-start.2 = (bf16[48,128]{1,0:T(8,128)(2,1)S(1)}, bf16[48,128]{1,0:T(8,128)(2,1)}, u32[]{:S(2)}) copy-start(bf16[48,128]{1,0:T(8,128)(2,1)} %get-tuple-element.11) | copy-start | bytes 36868
  3.4 14.3 %copy-start = (bf16[48,128]{1,0:T(8,128)(2,1)S(1)}, bf16[48,128]{1,0:T(8,128)(2,1)}, u32[]{:S(2)}) copy-start(bf16[48,128]{1,0:T(8,128)(2,1)} %get-tuple-element.10) | copy-start | bytes 36868
  3.5 49.0 %all-to-all-start = ((bf16[64,48,128]{2,1,0:T(8,128)(2,1)}), bf16[64,48,128]{2,1,0:T(8,128)(2,1)S(1)}, u32[]{:S(2)}, u32[]{:S(2)}) async-start(bf16[64,48,128]{2,1,0:T(8,128)(2,1)} %get-tuple-element.9), calls=%async_computation | async-start | bytes 1572864 | tf_op jit(solution)/shard_map/all_to_all | solution.py:306
  14.4 3.3 %collective-permute-start = (bf16[48,128]{1,0:T(8,128)(2,1)S(1)}, bf16[48,128]{1,0:T(8,128)(2,1)S(1)}, u32[]{:S(2)}, u32[]{:S(2)}) collective-permute-start(bf16[48,128]{1,0:T(8,128)(2,1)S(1)} %copy-done.2), channel_id=1, source_target_pairs={{0,16},{16,0},{1,17},{17,1},{2,18},{18,2},{3,19},{19,3},{4,20},{20... | collective-permute-start | bytes 36872 | tf_op jit(solution)/shard_map/ppermute | solution.py:334
  57.8 24.1 %all-to-all-start.1 = ((f32[8,56,128]{2,1,0:T(8,128)}), f32[8,56,128]{2,1,0:T(8,128)S(1)}, u32[]{:S(2)}, u32[]{:S(2)}) async-start(f32[8,56,128]{2,1,0:T(8,128)} %get-tuple-element.12), calls=%async_computation.1 | async-start | bytes 458752 | tf_op jit(solution)/shard_map/all_to_all | solution.py:306
  64.3 0.7 copy-start.1
  85.1 20.5 %all-to-all-start.2 = ((bf16[64,16,128]{2,1,0:T(8,128)(2,1)}), bf16[64,16,128]{2,1,0:T(8,128)(2,1)S(1)}, u32[]{:S(2)}, u32[]{:S(2)}) async-start(bf16[64,16,128]{2,1,0:T(8,128)(2,1)} %get-tuple-element.15), calls=%async_computation.2 | async-start | bytes 524288 | tf_op jit(solution)/shard_map/all_to_all | solution.py:306
  95.4 5.1 %collective-permute-start.1 = (f32[2,16,128]{2,1,0:T(8,128)S(1)}, f32[2,16,128]{2,1,0:T(8,128)S(1)}, u32[]{:S(2)}, u32[]{:S(2)}) collective-permute-start(f32[2,16,128]{2,1,0:T(8,128)S(1)} %slice.9), channel_id=1, source_target_pairs={{0,32},{32,0},{1,33},{33,1},{2,34},{34,2},{3,35},{35,3},{4,36},{36... | collective-permute-start | bytes 49160 | tf_op jit(solution)/shard_map/ppermute | solution.py:372
  100.5 3.7 %collective-permute-start.2 = (f32[2,16,128]{2,1,0:T(8,128)S(1)}, f32[2,16,128]{2,1,0:T(8,128)S(1)}, u32[]{:S(2)}, u32[]{:S(2)}) collective-permute-start(f32[2,16,128]{2,1,0:T(8,128)S(1)} %pad_maximum_fusion), channel_id=1, source_target_pairs={{0,16},{16,0},{1,17},{17,1},{2,18},{18,2},{3,19},{19,3},{4,20},{20... | collective-permute-start | bytes 49160 | tf_op jit(solution)/shard_map/ppermute | solution.py:372
